TPU v7x, 128 devices: a whole 4x4x4 slice. The times are simulated.
128 devices in a mesh: dp: 32 (over y, z, core), replica: 4 (over x).
Axes of the slice: x: 4, y: 4, z: 4, core: 2. Of those that a mesh axis runs over, the one named last changes fastest.
Arguments:
- replay: bfloat16 [1024, 24, 81, 232], P(('dp', 'replica')), may hold values from -6 to 6
- instructions: bfloat16 [1024, 512], P(('dp', 'replica')), may hold values from -6 to 6
- owners: int32 [4608, 1], P(('dp', 'replica')), may hold values from 0 to 31; in each aligned block of 36 rows (0 to 35, 36 to 71, ...) at most 3 rows name the same one
- episode_rows: int32 [4608], P(('dp', 'replica')), may hold values from 0 to 7
- frame_steps: int32 [4608], P(('dp', 'replica')), may hold values from 0 to 23
- w_expand: bfloat16 [232, 1392], replicated, may hold values from -0.375 to 0.375
- dw_kernel: float32 [9, 1392], replicated, may hold values from -2 to 2
- w_project: bfloat16 [1392, 384], replicated, may hold values from -0.15625 to 0.15625
- film_weight: bfloat16 [512, 768], replicated, may hold values from -0.25 to 0.25
- token_grad: bfloat16 [768, 6, 81, 384], P(('dp', 'replica')), may hold values from -0.0390625 to 0.0390625
Outputs:
- tokens: bfloat16 [768, 6, 81, 384], P(('dp', 'replica'))
- grad_expand: float32 [232, 1392], replicated
- grad_kernel: float32 [9, 1392], replicated
- grad_project: float32 [1392, 384], replicated
- grad_film: float32 [512, 768], replicated
Inputs may be any that keep to these rules, and one draw needn't show every extreme that they name: `owners`: among the 36 request rows of one device, no owner is named more than 3 times, and some device names some owner exactly 3 times.
All inputs are finite; a program needn't handle non-finite values.
Results may differ from a plain program's by a relative error of at most 0.006.
Values may be sent and summed in bfloat16 or wider, within the bound.
A program may use at most 448 MiB of HBM per device.

v0:
```python
import jax
import jax.numpy as jnp
from jax import lax
from jax.sharding import PartitionSpec as P

SIDE = 9


def silu_parts(values):
    sigmoid_value = jax.nn.sigmoid(values)
    return (values * sigmoid_value, sigmoid_value * (1.0 + values * (1.0 - sigmoid_value)))


def depthwise(grid_values, dw_kernel):
    padded = jnp.pad(grid_values, ((0, 0), (1, 1), (1, 1), (0, 0)))
    result = jnp.zeros_like(grid_values)
    for kernel_tap in range(9):
        tap_row, tap_col = (kernel_tap // 3, kernel_tap % 3)
        result = (
            result
            + dw_kernel[kernel_tap]
            * padded[:, tap_row : tap_row + SIDE, tap_col : tap_col + SIDE, :]
        )
    return result


def depthwise_back(mixed_cot, source_grid, dw_kernel):
    padded_source = jnp.pad(source_grid, ((0, 0), (1, 1), (1, 1), (0, 0)))
    padded_cot = jnp.pad(mixed_cot, ((0, 0), (1, 1), (1, 1), (0, 0)))
    kernel_rows = []
    result = jnp.zeros_like(mixed_cot)
    for kernel_tap in range(9):
        tap_row, tap_col = (kernel_tap // 3, kernel_tap % 3)
        window = padded_source[:, tap_row : tap_row + SIDE, tap_col : tap_col + SIDE, :]
        kernel_rows.append(jnp.sum(mixed_cot * window, axis=(0, 1, 2)))
        result = (
            result
            + dw_kernel[kernel_tap]
            * padded_cot[:, 2 - tap_row : 2 - tap_row + SIDE, 2 - tap_col : 2 - tap_col + SIDE, :]
        )
    return (jnp.stack(kernel_rows), result)


def forward(frames, embedding, w_expand, dw_kernel, w_project, film_weight):
    amount, cell_count, in_width = frames.shape
    out_width = w_project.shape[1]
    before = jnp.dot(
        frames.reshape(amount * cell_count, in_width), w_expand, preferred_element_type=jnp.float32
    )
    first_act, first_slope = silu_parts(before)
    first_hidden = lax.optimization_barrier(first_act.astype(jnp.bfloat16))
    mixed = depthwise(first_hidden.astype(jnp.float32).reshape(amount, SIDE, SIDE, -1), dw_kernel)
    second_act, second_slope = silu_parts(mixed)
    second_hidden = second_act.astype(jnp.bfloat16).reshape(amount * cell_count, -1)
    projected = jnp.dot(second_hidden, w_project, preferred_element_type=jnp.float32).reshape(
        amount, cell_count, out_width
    )
    film_terms = jnp.dot(embedding, film_weight, preferred_element_type=jnp.float32)
    film_scale = 1.0 + film_terms[:, None, :out_width]
    film_shift = film_terms[:, None, out_width:]
    tokens = (film_scale * projected + film_shift).astype(jnp.bfloat16)
    saved = (
        first_hidden.reshape(amount, cell_count, -1),
        first_slope.reshape(amount, cell_count, -1),
        second_hidden.reshape(amount, cell_count, -1),
        second_slope.reshape(amount, cell_count, -1),
        projected,
    )
    return (tokens, saved)


def backward(frames, embedding, saved, cotangent, dw_kernel, w_project, film_weight):
    amount, cell_count, in_width = frames.shape
    out_width = w_project.shape[1]
    first_hidden, first_slope, second_hidden, second_slope, projected = saved
    contract_rows = (((0,), (0,)), ((), ()))
    film_terms = jnp.dot(embedding, film_weight, preferred_element_type=jnp.float32)
    film_scale = 1.0 + film_terms[:, None, :out_width]
    upstream = cotangent.astype(jnp.float32)
    film_cot = jnp.concatenate(
        [jnp.sum(upstream * projected, axis=1), jnp.sum(upstream, axis=1)], axis=1
    ).astype(jnp.bfloat16)
    film_grad = lax.dot_general(
        embedding, film_cot, contract_rows, preferred_element_type=jnp.float32
    )
    proj_cot = (upstream * film_scale).astype(jnp.bfloat16).reshape(amount * cell_count, out_width)
    first_grid = first_hidden.astype(jnp.float32).reshape(amount, SIDE, SIDE, -1)
    flat_second = second_hidden.reshape(amount * cell_count, -1)
    project_grad = lax.dot_general(
        flat_second, proj_cot, contract_rows, preferred_element_type=jnp.float32
    )
    second_cot = lax.dot_general(
        proj_cot, w_project, (((1,), (1,)), ((), ())), preferred_element_type=jnp.float32
    )
    mixed_cot = second_cot.reshape(amount, SIDE, SIDE, -1) * second_slope.reshape(
        amount, SIDE, SIDE, -1
    )
    kernel_grad, first_cot = depthwise_back(mixed_cot, first_grid, dw_kernel)
    flat_frames = frames.reshape(amount * cell_count, in_width)
    pre_cot = (
        first_cot.reshape(amount * cell_count, -1) * first_slope.reshape(amount * cell_count, -1)
    ).astype(jnp.bfloat16)
    expand_grad = lax.dot_general(
        flat_frames, pre_cot, contract_rows, preferred_element_type=jnp.float32
    )
    return (expand_grad, kernel_grad, project_grad, film_grad)


def block_frames(amount):
    return max((divisor for divisor in range(1, 9) if amount % divisor == 0))


def forward_blocks(frames, embedding, w_expand, dw_kernel, w_project, film_weight):
    amount, cell_count, in_width = frames.shape
    stride = block_frames(amount)
    groups = amount // stride

    def forward_one_block(pieces):
        return forward(pieces[0], pieces[1], w_expand, dw_kernel, w_project, film_weight)

    tokens, saved = lax.map(
        forward_one_block,
        (
            frames.reshape(groups, stride, cell_count, in_width),
            embedding.reshape(groups, stride, -1),
        ),
    )

    def flatten(values):
        return values.reshape((amount,) + values.shape[2:])

    return (flatten(tokens), jax.tree.map(flatten, saved))


def backward_blocks(
    frames, embedding, saved, cotangent, w_expand, dw_kernel, w_project, film_weight
):
    amount = frames.shape[0]
    stride = block_frames(amount)
    groups = amount // stride

    def regroup(values):
        return values.reshape((groups, stride) + values.shape[1:])

    def backward_one_block(totals, pieces):
        fresh = backward(
            pieces[0], pieces[1], pieces[2], pieces[3], dw_kernel, w_project, film_weight
        )
        return (tuple((left + right for left, right in zip(totals, fresh))), None)

    start_totals = (
        jnp.zeros(w_expand.shape, jnp.float32),
        jnp.zeros(dw_kernel.shape, jnp.float32),
        jnp.zeros(w_project.shape, jnp.float32),
        jnp.zeros(film_weight.shape, jnp.float32),
    )
    gradients, unused = lax.scan(
        backward_one_block,
        start_totals,
        (regroup(frames), regroup(embedding), jax.tree.map(regroup, saved), regroup(cotangent)),
    )
    return gradients


def reduce_gradients(gradients):
    return lax.psum((gradients[0], gradients[1], gradients[2], gradients[3]), ("dp", "replica"))


def per_device(
    replay,
    instructions,
    owners,
    episode_rows,
    frame_steps,
    w_expand,
    dw_kernel,
    w_project,
    film_weight,
    token_grad,
):
    peer_count = lax.axis_size("dp")
    frame_count = owners.shape[0]
    capacity = max(2, (2 * frame_count + peer_count - 1) // peer_count)
    slot_count = peer_count * capacity
    episode_length = replay.shape[1]
    cell_count = replay.shape[2]
    out_width = w_project.shape[1]
    owner_ids = owners[:, 0]
    positions = jnp.arange(frame_count, dtype=jnp.int32)
    earlier = (owner_ids[:, None] == owner_ids[None, :]) & (positions[:, None] < positions[None, :])
    rank_within = jnp.sum(earlier.astype(jnp.int32), axis=0)
    target = owner_ids * capacity + rank_within
    onehot = target[:, None] == jnp.arange(slot_count, dtype=jnp.int32)[None, :]
    wanted = episode_rows * episode_length + frame_steps
    request = jnp.sum(jnp.where(onehot, wanted[:, None], 0), axis=0).reshape(peer_count, capacity)
    asked_rows = lax.all_to_all(request, "dp", split_axis=0, concat_axis=0, tiled=True).reshape(
        slot_count
    )
    stored = replay.reshape(-1, cell_count, replay.shape[3])
    picked = jnp.take(stored, asked_rows, axis=0)
    picked_embedding = jnp.take(instructions, asked_rows // episode_length, axis=0)
    arrived, arrived_embedding = (
        lax.all_to_all(
            picked.reshape(peer_count, capacity, cell_count, -1),
            "dp",
            split_axis=0,
            concat_axis=0,
            tiled=True,
        ),
        lax.all_to_all(
            picked_embedding.reshape(peer_count, capacity, -1),
            "dp",
            split_axis=0,
            concat_axis=0,
            tiled=True,
        ),
    )
    frames = jnp.take(arrived.reshape(slot_count, cell_count, -1), target, axis=0)
    embedding = jnp.take(arrived_embedding.reshape(slot_count, -1), target, axis=0)
    tokens, saved = forward_blocks(frames, embedding, w_expand, dw_kernel, w_project, film_weight)
    tokens_out = tokens.reshape(token_grad.shape)
    cotangent = token_grad.reshape(frame_count, cell_count, out_width)
    gradients = backward_blocks(
        frames, embedding, saved, cotangent, w_expand, dw_kernel, w_project, film_weight
    )
    summed = reduce_gradients(gradients)
    return (tokens_out, summed[0], summed[1], summed[2], summed[3])


def solution(mesh):
    in_specs = (
        P(("dp", "replica"), None, None, None),
        P(("dp", "replica"), None),
        P(("dp", "replica"), None),
        P(("dp", "replica")),
        P(("dp", "replica")),
        P(),
        P(),
        P(),
        P(),
        P(("dp", "replica"), None, None, None),
    )
    out_specs = (P(("dp", "replica"), None, None, None), P(), P(), P(), P())
    return jax.shard_map(
        per_device, mesh=mesh, in_specs=in_specs, out_specs=out_specs, check_vma=False
    )
```

profile of v0, /device:TPU:1, one launch (start us, length us, event | category | flops | bytes accessed | tf_op | source)
XLA Modules:
  0.0 1069.2 jit_solution(1950980877483898079)
XLA Ops:
  10.1 9.6 all-to-all-start
  19.8 7.5 copy.89
  27.2 11.1 %copy.90 = bf16[192,81,232]{2,1,0:T(8,128)(2,1)} copy(bf16[192,81,232]{2,0,1:T(8,128)(2,1)} %bitcast.134) | data formatting | bytes 14432256 | tf_op jit(solution)/shard_map/reshape | solution.py:199
  41.7 7.4 all-to-all-start.1
  49.0 6.5 gather_fusion.2
  55.5 4.7 broadcast_select_fusion
  60.2 7.6 all-to-all-start.2
  69.1 52.5 %all-to-all-done.2 = bf16[32,3,81,232]{3,2,1,0:T(8,128)(2,1)} async-done(((bf16[32,3,81,232]{3,2,1,0:T(8,128)(2,1)}), bf16[32,3,81,232]{3,2,1,0:T(8,128)(2,1)}, u32[]{:S(2)}, u32[]{:S(2)}) %all-to-all-start.2) | async-done | bytes 3608096 | tf_op jit(solution)/shard_map/all_to_all | solution.py:203
  125.9 347.5 %while.41 = (s32[]{:T(128)}, bf16[6,6,81,384]{3,2,1,0:T(8,128)(2,1)}, bf16[6,6,81,1392]{3,2,1,0:T(8,128)(2,1)}, f32[6,6,81,1392]{3,2,1,0:T(8,128)}, bf16[6,6,81,...) while((s32[]{:T(128)}, ...), condition=%wide.region_3.4_spmd, body=%wide.region_2.3_spmd.sunk | while | flops 864451008 | bytes 73136328 | solution.py:121
  133.8 23.1 %add_multiply_fusion.5 = (f32[6,9,9,1392]{3,2,1,0:T(8,128)}, f32[6,9,9,1392]{3,2,1,0:T(8,128)S(1)}) fusion(f32[1392]{0:T(1024)S(1)} %get-tuple-element.861, f32[1392]{0:T(1024)S(1)} %get-tuple-element.862, f32[1392]{0:T(1024)S(1)} %get-tuple-element.863, f32[1392]{0:T(1024)S(1)} %get-tuple-element.864, f32[6,9,9,1392]{3,2,1,0:T(8,128)} %reshape.400, ...), kind=kLoop, calls=%fused_computation.28.clone.1 | loop fusion | flops 16236288 | bytes 8168256 | tf_op jit(solution)/shard_map/while/body/eval_jaxpr/mul | solution.py:11
  191.6 23.1 %add_multiply_fusion.5 = (f32[6,9,9,1392]{3,2,1,0:T(8,128)}, f32[6,9,9,1392]{3,2,1,0:T(8,128)S(1)}) fusion(f32[1392]{0:T(1024)S(1)} %get-tuple-element.861, f32[1392]{0:T(1024)S(1)} %get-tuple-element.862, f32[1392]{0:T(1024)S(1)} %get-tuple-element.863, f32[1392]{0:T(1024)S(1)} %get-tuple-element.864, f32[6,9,9,1392]{3,2,1,0:T(8,128)} %reshape.400, ...), kind=kLoop, calls=%fused_computation.28.clone.1 | loop fusion | flops 16236288 | bytes 8168256 | tf_op jit(solution)/shard_map/while/body/eval_jaxpr/mul | solution.py:11
  249.7 23.1 %add_multiply_fusion.5 = (f32[6,9,9,1392]{3,2,1,0:T(8,128)}, f32[6,9,9,1392]{3,2,1,0:T(8,128)S(1)}) fusion(f32[1392]{0:T(1024)S(1)} %get-tuple-element.861, f32[1392]{0:T(1024)S(1)} %get-tuple-element.862, f32[1392]{0:T(1024)S(1)} %get-tuple-element.863, f32[1392]{0:T(1024)S(1)} %get-tuple-element.864, f32[6,9,9,1392]{3,2,1,0:T(8,128)} %reshape.400, ...), kind=kLoop, calls=%fused_computation.28.clone.1 | loop fusion | flops 16236288 | bytes 8168256 | tf_op jit(solution)/shard_map/while/body/eval_jaxpr/mul | solution.py:11
  307.8 23.1 %add_multiply_fusion.5 = (f32[6,9,9,1392]{3,2,1,0:T(8,128)}, f32[6,9,9,1392]{3,2,1,0:T(8,128)S(1)}) fusion(f32[1392]{0:T(1024)S(1)} %get-tuple-element.861, f32[1392]{0:T(1024)S(1)} %get-tuple-element.862, f32[1392]{0:T(1024)S(1)} %get-tuple-element.863, f32[1392]{0:T(1024)S(1)} %get-tuple-element.864, f32[6,9,9,1392]{3,2,1,0:T(8,128)} %reshape.400, ...), kind=kLoop, calls=%fused_computation.28.clone.1 | loop fusion | flops 16236288 | bytes 8168256 | tf_op jit(solution)/shard_map/while/body/eval_jaxpr/mul | solution.py:11
  365.7 23.1 %add_multiply_fusion.5 = (f32[6,9,9,1392]{3,2,1,0:T(8,128)}, f32[6,9,9,1392]{3,2,1,0:T(8,128)S(1)}) fusion(f32[1392]{0:T(1024)S(1)} %get-tuple-element.861, f32[1392]{0:T(1024)S(1)} %get-tuple-element.862, f32[1392]{0:T(1024)S(1)} %get-tuple-element.863, f32[1392]{0:T(1024)S(1)} %get-tuple-element.864, f32[6,9,9,1392]{3,2,1,0:T(8,128)} %reshape.400, ...), kind=kLoop, calls=%fused_computation.28.clone.1 | loop fusion | flops 16236288 | bytes 8168256 | tf_op jit(solution)/shard_map/while/body/eval_jaxpr/mul | solution.py:11
  423.5 23.1 %add_multiply_fusion.5 = (f32[6,9,9,1392]{3,2,1,0:T(8,128)}, f32[6,9,9,1392]{3,2,1,0:T(8,128)S(1)}) fusion(f32[1392]{0:T(1024)S(1)} %get-tuple-element.861, f32[1392]{0:T(1024)S(1)} %get-tuple-element.862, f32[1392]{0:T(1024)S(1)} %get-tuple-element.863, f32[1392]{0:T(1024)S(1)} %get-tuple-element.864, f32[6,9,9,1392]{3,2,1,0:T(8,128)} %reshape.400, ...), kind=kLoop, calls=%fused_computation.28.clone.1 | loop fusion | flops 16236288 | bytes 8168256 | tf_op jit(solution)/shard_map/while/body/eval_jaxpr/mul | solution.py:11
  473.4 424.9 %while.42 = (s32[]{:T(128)}, f32[232,1392]{1,0:T(8,128)}, f32[9,1392]{1,0:T(8,128)S(1)}, f32[1392,384]{1,0:T(8,128)}, f32[512,768]{1,0:T(8,128)}, /*index=5*/bf1...) while((s32[]{:T(128)}, f32[232,1392]{1,0:T(8,128)}, ...), condition=%wide.region_16.17_spmd.clone, body=%wide.region_4.16_spmd.clone.sunk | while | flops 1390695424 | bytes 88002440 | solution.py:157
  483.1 4.0 constant_dynamic-slice_fusion.18
  487.1 12.6 %fusion.130 = (f32[1392]{0:T(1024)S(1)}, f32[1392]{0:T(1024)S(1)}, f32[1392]{0:T(1024)}, f32[1392]{0:T(1024)}, f32[1392]{0:T(1024)}, /*index=5*/f32[1392]{0:T(10...) fusion(f32[6,9,9,1392]{3,2,1,0:T(8,128)S(1)} %copy.145, ...), kind=kOutput, calls=%fused_computation.105.clone.1 | convolution fusion | flops 532402304 | bytes 12316608 | tf_op jit(solution)/shard_map/while/body/eval_jaxpr/dot_general | solution.py:92
  507.7 21.3 %fusion.131 = bf16[6,9,9,1392]{3,2,1,0:T(8,128)(2,1)S(1)} fusion(f32[6,9,9,1392]{3,2,1,0:T(8,128)} %get-tuple-element.896, f32[6,9,9,1392]{3,0,2,1:T(8,128)S(1)} %bitcast.129, f32[1392]{0:T(1024)S(1)} %get-tuple-element.897, f32[1392]{0:T(1024)S(1)} %get-tuple-element.898, f32[1392]{0:T(1024)S(1)} %get-tuple-element.899, ...), kind=kLoop, calls=%fused_computation.82.clone.1 | loop fusion | flops 12853728 | bytes 6815232 | tf_op jit(solution)/shard_map/while/body/eval_jaxpr/convert_element_type | solution.py:102
  551.1 4.0 constant_dynamic-slice_fusion.18
  555.1 12.6 %fusion.130 = (f32[1392]{0:T(1024)S(1)}, f32[1392]{0:T(1024)S(1)}, f32[1392]{0:T(1024)}, f32[1392]{0:T(1024)}, f32[1392]{0:T(1024)}, /*index=5*/f32[1392]{0:T(10...) fusion(f32[6,9,9,1392]{3,2,1,0:T(8,128)S(1)} %copy.145, ...), kind=kOutput, calls=%fused_computation.105.clone.1 | convolution fusion | flops 532402304 | bytes 12316608 | tf_op jit(solution)/shard_map/while/body/eval_jaxpr/dot_general | solution.py:92
  575.6 21.3 %fusion.131 = bf16[6,9,9,1392]{3,2,1,0:T(8,128)(2,1)S(1)} fusion(f32[6,9,9,1392]{3,2,1,0:T(8,128)} %get-tuple-element.896, f32[6,9,9,1392]{3,0,2,1:T(8,128)S(1)} %bitcast.129, f32[1392]{0:T(1024)S(1)} %get-tuple-element.897, f32[1392]{0:T(1024)S(1)} %get-tuple-element.898, f32[1392]{0:T(1024)S(1)} %get-tuple-element.899, ...), kind=kLoop, calls=%fused_computation.82.clone.1 | loop fusion | flops 12853728 | bytes 6815232 | tf_op jit(solution)/shard_map/while/body/eval_jaxpr/convert_element_type | solution.py:102
  626.5 12.6 %fusion.130 = (f32[1392]{0:T(1024)S(1)}, f32[1392]{0:T(1024)S(1)}, f32[1392]{0:T(1024)}, f32[1392]{0:T(1024)}, f32[1392]{0:T(1024)}, /*index=5*/f32[1392]{0:T(10...) fusion(f32[6,9,9,1392]{3,2,1,0:T(8,128)S(1)} %copy.145, ...), kind=kOutput, calls=%fused_computation.105.clone.1 | convolution fusion | flops 532402304 | bytes 12316608 | tf_op jit(solution)/shard_map/while/body/eval_jaxpr/dot_general | solution.py:92
  647.0 21.3 %fusion.131 = bf16[6,9,9,1392]{3,2,1,0:T(8,128)(2,1)S(1)} fusion(f32[6,9,9,1392]{3,2,1,0:T(8,128)} %get-tuple-element.896, f32[6,9,9,1392]{3,0,2,1:T(8,128)S(1)} %bitcast.129, f32[1392]{0:T(1024)S(1)} %get-tuple-element.897, f32[1392]{0:T(1024)S(1)} %get-tuple-element.898, f32[1392]{0:T(1024)S(1)} %get-tuple-element.899, ...), kind=kLoop, calls=%fused_computation.82.clone.1 | loop fusion | flops 12853728 | bytes 6815232 | tf_op jit(solution)/shard_map/while/body/eval_jaxpr/convert_element_type | solution.py:102
  697.9 12.6 %fusion.130 = (f32[1392]{0:T(1024)S(1)}, f32[1392]{0:T(1024)S(1)}, f32[1392]{0:T(1024)}, f32[1392]{0:T(1024)}, f32[1392]{0:T(1024)}, /*index=5*/f32[1392]{0:T(10...) fusion(f32[6,9,9,1392]{3,2,1,0:T(8,128)S(1)} %copy.145, ...), kind=kOutput, calls=%fused_computation.105.clone.1 | convolution fusion | flops 532402304 | bytes 12316608 | tf_op jit(solution)/shard_map/while/body/eval_jaxpr/dot_general | solution.py:92
  718.4 21.3 %fusion.131 = bf16[6,9,9,1392]{3,2,1,0:T(8,128)(2,1)S(1)} fusion(f32[6,9,9,1392]{3,2,1,0:T(8,128)} %get-tuple-element.896, f32[6,9,9,1392]{3,0,2,1:T(8,128)S(1)} %bitcast.129, f32[1392]{0:T(1024)S(1)} %get-tuple-element.897, f32[1392]{0:T(1024)S(1)} %get-tuple-element.898, f32[1392]{0:T(1024)S(1)} %get-tuple-element.899, ...), kind=kLoop, calls=%fused_computation.82.clone.1 | loop fusion | flops 12853728 | bytes 6815232 | tf_op jit(solution)/shard_map/while/body/eval_jaxpr/convert_element_type | solution.py:102
  769.3 12.6 %fusion.130 = (f32[1392]{0:T(1024)S(1)}, f32[1392]{0:T(1024)S(1)}, f32[1392]{0:T(1024)}, f32[1392]{0:T(1024)}, f32[1392]{0:T(1024)}, /*index=5*/f32[1392]{0:T(10...) fusion(f32[6,9,9,1392]{3,2,1,0:T(8,128)S(1)} %copy.145, ...), kind=kOutput, calls=%fused_computation.105.clone.1 | convolution fusion | flops 532402304 | bytes 12316608 | tf_op jit(solution)/shard_map/while/body/eval_jaxpr/dot_general | solution.py:92
  789.8 21.3 %fusion.131 = bf16[6,9,9,1392]{3,2,1,0:T(8,128)(2,1)S(1)} fusion(f32[6,9,9,1392]{3,2,1,0:T(8,128)} %get-tuple-element.896, f32[6,9,9,1392]{3,0,2,1:T(8,128)S(1)} %bitcast.129, f32[1392]{0:T(1024)S(1)} %get-tuple-element.897, f32[1392]{0:T(1024)S(1)} %get-tuple-element.898, f32[1392]{0:T(1024)S(1)} %get-tuple-element.899, ...), kind=kLoop, calls=%fused_computation.82.clone.1 | loop fusion | flops 12853728 | bytes 6815232 | tf_op jit(solution)/shard_map/while/body/eval_jaxpr/convert_element_type | solution.py:102
  840.6 12.6 %fusion.130 = (f32[1392]{0:T(1024)S(1)}, f32[1392]{0:T(1024)S(1)}, f32[1392]{0:T(1024)}, f32[1392]{0:T(1024)}, f32[1392]{0:T(1024)}, /*index=5*/f32[1392]{0:T(10...) fusion(f32[6,9,9,1392]{3,2,1,0:T(8,128)S(1)} %copy.145, ...), kind=kOutput, calls=%fused_computation.105.clone.1 | convolution fusion | flops 532402304 | bytes 12316608 | tf_op jit(solution)/shard_map/while/body/eval_jaxpr/dot_general | solution.py:92
  861.2 21.3 %fusion.131 = bf16[6,9,9,1392]{3,2,1,0:T(8,128)(2,1)S(1)} fusion(f32[6,9,9,1392]{3,2,1,0:T(8,128)} %get-tuple-element.896, f32[6,9,9,1392]{3,0,2,1:T(8,128)S(1)} %bitcast.129, f32[1392]{0:T(1024)S(1)} %get-tuple-element.897, f32[1392]{0:T(1024)S(1)} %get-tuple-element.898, f32[1392]{0:T(1024)S(1)} %get-tuple-element.899, ...), kind=kLoop, calls=%fused_computation.82.clone.1 | loop fusion | flops 12853728 | bytes 6815232 | tf_op jit(solution)/shard_map/while/body/eval_jaxpr/convert_element_type | solution.py:102
  898.3 68.0 %psum.29 = f32[9,1392]{1,0:T(8,128)} all-reduce(f32[9,1392]{1,0:T(8,128)S(1)} %get-tuple-element.378), channel_id=1, replica_groups=mesh['dp'=32,'replica'=4] {'dp','replica'}, use_global_device_ids=true, to_apply=%region_18.19 | all-reduce | flops 12528 | bytes 100224 | tf_op jit(solution)/shard_map/psum | solution.py:166
  966.3 89.2 %all-reduce.6.cloned.1.call-done = (f32[232,1392]{1,0:T(8,128)}, f32[1392,384]{1,0:T(8,128)}, f32[512,768]{1,0:T(8,128)}) async-done(((f32[232,1392]{1,0:T(8,128)}, f32[1392,384]{1,0:T(8,128)}, f32[512,768]{1,0:T(8,128)}), (f32[232,1392]{1,0:T(8,128)}, f32[1392,384]{1,0:T(8,128)}, f32[512,768]{1,0:T(8,128)})) %all-reduce.6.cloned.1.call-update) | async-done | bytes 5002768 | tf_op jit(solution)/shard_map/psum | solution.py:166
  (423 shorter events, 440.2 us)
Async XLA Ops:
  7.2 32.7 %copy-start = (bf16[8,512]{1,0:T(8,128)(2,1)S(1)}, bf16[8,512]{1,0:T(8,128)(2,1)}, u32[]{:S(2)}) copy-start(bf16[8,512]{1,0:T(8,128)(2,1)} %param.15) | copy-start | bytes 24580
  10.1 28.2 %all-to-all-start = ((s32[32,1,3]{2,1,0:T(1,128)}), s32[32,1,3]{2,1,0:T(1,128)S(1)}, u32[]{:S(2)}, u32[]{:S(2)}) async-start(s32[32,1,3]{2,1,0:T(1,128)} %bitcast.6), calls=%async_computation | async-start | bytes 32768 | tf_op jit(solution)/shard_map/all_to_all | solution.py:196
  41.7 18.5 %all-to-all-start.1 = ((bf16[32,3,512]{2,1,0:T(4,128)(2,1)}), bf16[32,3,512]{2,1,0:T(4,128)(2,1)S(1)}, u32[]{:S(2)}, u32[]{:S(2)}) async-start(bf16[32,3,512]{2,1,0:T(4,128)(2,1)} %broadcast_select_fusion.2), calls=%async_computation.1 | async-start | bytes 262144 | tf_op jit(solution)/shard_map/all_to_all | solution.py:210
  60.2 7.9 copy-start.8
  60.2 61.4 %all-to-all-start.2 = ((bf16[32,3,81,232]{3,2,1,0:T(8,128)(2,1)}), bf16[32,3,81,232]{3,2,1,0:T(8,128)(2,1)}, u32[]{:S(2)}, u32[]{:S(2)}) async-start(bf16[32,3,81,232]{3,2,1,0:T(8,128)(2,1)} %broadcast_select_fusion), calls=%async_computation.2 | async-start | bytes 8650752 | tf_op jit(solution)/shard_map/all_to_all | solution.py:203
  67.8 58.1 %copy-start.6 = (f32[9,1392]{1,0:T(8,128)S(1)}, f32[9,1392]{1,0:T(8,128)}, u32[]{:S(2)}) copy-start(f32[9,1392]{1,0:T(8,128)} %param.20) | copy-start | bytes 150340
  67.8 987.7 %all-reduce.6.cloned.1.call-start = ((), (), s32[]{:S(2)}) async-start(), calls=%async_computation.3 | async-start | bytes 10035200 | tf_op jit(solution)/shard_map/psum | solution.py:166
  130.9 26.0 %copy-start.3 = (bf16[486,1392]{1,0:T(8,128)(2,1)}, bf16[486,1392]{1,0:T(8,128)(2,1)S(1)}, u32[]{:S(2)}) copy-start(bf16[486,1392]{1,0:T(8,128)(2,1)S(1)} %get-tuple-element.865) | copy-start | bytes 4059076 | tf_op jit(solution)/shard_map/while
  188.7 26.0 %copy-start.3 = (bf16[486,1392]{1,0:T(8,128)(2,1)}, bf16[486,1392]{1,0:T(8,128)(2,1)S(1)}, u32[]{:S(2)}) copy-start(bf16[486,1392]{1,0:T(8,128)(2,1)S(1)} %get-tuple-element.865) | copy-start | bytes 4059076 | tf_op jit(solution)/shard_map/while
  246.7 26.0 %copy-start.3 = (bf16[486,1392]{1,0:T(8,128)(2,1)}, bf16[486,1392]{1,0:T(8,128)(2,1)S(1)}, u32[]{:S(2)}) copy-start(bf16[486,1392]{1,0:T(8,128)(2,1)S(1)} %get-tuple-element.865) | copy-start | bytes 4059076 | tf_op jit(solution)/shard_map/while
  304.8 26.0 %copy-start.3 = (bf16[486,1392]{1,0:T(8,128)(2,1)}, bf16[486,1392]{1,0:T(8,128)(2,1)S(1)}, u32[]{:S(2)}) copy-start(bf16[486,1392]{1,0:T(8,128)(2,1)S(1)} %get-tuple-element.865) | copy-start | bytes 4059076 | tf_op jit(solution)/shard_map/while
  362.8 26.0 %copy-start.3 = (bf16[486,1392]{1,0:T(8,128)(2,1)}, bf16[486,1392]{1,0:T(8,128)(2,1)S(1)}, u32[]{:S(2)}) copy-start(bf16[486,1392]{1,0:T(8,128)(2,1)S(1)} %get-tuple-element.865) | copy-start | bytes 4059076 | tf_op jit(solution)/shard_map/while
  420.5 26.0 %copy-start.3 = (bf16[486,1392]{1,0:T(8,128)(2,1)}, bf16[486,1392]{1,0:T(8,128)(2,1)S(1)}, u32[]{:S(2)}) copy-start(bf16[486,1392]{1,0:T(8,128)(2,1)S(1)} %get-tuple-element.865) | copy-start | bytes 4059076 | tf_op jit(solution)/shard_map/while
  475.7 0.8 copy-start.4
  529.0 7.4 copy-start.5
  535.0 3.3 copy-start.2
  543.6 0.8 copy-start.4
  597.0 7.8 copy-start.5
  603.4 4.8 copy-start.2
  615.0 0.8 copy-start.4
  668.3 7.8 copy-start.5
  674.8 4.8 copy-start.2
  686.4 0.8 copy-start.4
  739.7 7.8 copy-start.5
  746.2 4.8 copy-start.2
  757.8 0.8 copy-start.4
  811.1 7.8 copy-start.5
  817.5 4.8 copy-start.2
  882.5 7.8 copy-start.5
  888.9 4.8 copy-start.2
  1055.5 5.7 copy-start.7
  1055.5 6.8 copy-start.1
  (1 other events, 0.8 us)
Sparse Core Ops, SparseCore 0:
  898.4 157.0 all-reduce.5
where the time goes:
time: 1080 us; the launch traced here: 1070 us
  local copies, waits for them, and re-layouts  316 us (29%)
  other arithmetic  316 us (29%)
  matrix products  187 us (17%)
  waiting for transfers between devices  142 us (13%)
  blocking collectives  68 us (6%)
  starting transfers between devices  24.8 us (2%)
  between operations  14.2 us (1%)
    mul x6, other arithmetic, silu_parts(): sigmoid_value * (1.0 + values * (1.0 - sigmoid_value))  138 us
    convert_element_type x6, other arithmetic, backward(): pre_cot = (first_cot.reshape(amount * cell_count, -1) * first_slope.resha...  128 us
    psum x1, waiting for transfers between devices, reduce_gradients(): lax.psum((gradients[0], gradients[1], gradients[2], gradients[3]), ('dp',...  89.2 us
    dot_general x6, matrix products, backward(): lax.dot_general(proj_cot, w_project, (((1,), (1,)), ((), ())), preferred_...  75.3 us
    dynamic_slice x36, local copies, waits for them, and re-layouts, backward_blocks(): lax.scan(backward_one_block, start_totals, (regroup(frames), regroup(embe...  68.8 us
    psum x1, blocking collectives, reduce_gradients(): lax.psum((gradients[0], gradients[1], gradients[2], gradients[3]), ('dp',...  68 us
    all_to_all x1, waiting for transfers between devices, per_device(): lax.all_to_all(picked.reshape(peer_count, capacity, cell_count, -1), 'dp'...  52.5 us
    dynamic_update_slice x24, local copies, waits for them, and re-layouts, forward_blocks(): lax.map(forward_one_block, (frames.reshape(groups, stride, cell_count, in...  51.6 us
  transfers between devices with their start and end apart: 4, of which 2 were waited for; matrix products, arithmetic and copies ran while one was open for 3% of the time, Pallas kernels for 0%

commit v1 on v0

v1 whole, which is shorter than its diff:
```python
import jax, jax.numpy as jnp
from jax import lax
from jax.experimental import pallas as pl
from jax.experimental.pallas import tpu as pltpu
from jax.sharding import PartitionSpec as P

SIDE, CELLS, TILE = 9, 81, 8
CIN, HID, COUT, EMB, FR = 232, 1392, 384, 512, 36
HP = 1408
NT = 5
ROWS = CELLS * TILE
f32, bf16 = jnp.float32, jnp.bfloat16


def vpu_block(lane, tile_pre, tile_sc, dw_ref, F, S1, M, sec, prec, gk_ref):
    ln = pl.ds(lane, 128)
    row = lambda c: slice(c * 8, c * 8 + 8)
    for c in range(CELLS):
        h = tile_pre[row(c), ln]
        t = jnp.tanh(h)
        u = 1.0 + t
        F[row(c), :] = h * u
        S1[row(c), :] = u * (1.0 + h * (1.0 - t))
    taps = [dw_ref[t * 8:t * 8 + 8, ln] for t in range(9)]
    acc = [gk_ref[t * 8:t * 8 + 8, ln] for t in range(9)]
    get = lambda ref, i: [ref[row(i * 9 + k), :] for k in range(9)]
    prev, cur, nxt = None, None, get(F, 0)
    for i in range(9):
        prev, cur = cur, nxt
        nxt = get(F, i + 1) if i < 8 else None
        rows3 = (prev, cur, nxt)
        for k in range(9):
            total = None
            for r in range(3):
                if rows3[r] is None:
                    continue
                for c in range(3):
                    kk = k + c - 1
                    if 0 <= kk < 9:
                        term = taps[3 * r + c] * rows3[r][kk]
                        total = term if total is None else total + term
            h = total
            t = jnp.tanh(h)
            u = 1.0 + t
            sec[row(i * 9 + k), ln] = h * u
            mc = tile_sc[row(i * 9 + k), ln] * (u * (1.0 + h * (1.0 - t)))
            M[row(i * 9 + k), :] = mc
            for r in range(3):
                if rows3[r] is None:
                    continue
                for c in range(3):
                    kk = k + c - 1
                    if 0 <= kk < 9:
                        acc[3 * r + c] = acc[3 * r + c] + mc * rows3[r][kk]
    for t in range(9):
        gk_ref[t * 8:t * 8 + 8, ln] = acc[t]
    prev, cur, nxt = None, None, get(M, 0)
    for i in range(9):
        prev, cur = cur, nxt
        nxt = get(M, i + 1) if i < 8 else None
        rows3 = (nxt, cur, prev)
        for k in range(9):
            total = None
            for r in range(3):
                if rows3[r] is None:
                    continue
                for c in range(3):
                    kk = k - c + 1
                    if 0 <= kk < 9:
                        term = taps[3 * r + c] * rows3[r][kk]
                        total = term if total is None else total + term
            prec[row(i * 9 + k), ln] = total * S1[row(i * 9 + k), :]


def kernel(x_ref, e_ref, g_ref, we_ref, dw_ref, wp_ref, wpt_ref, fw_ref,
           tok_ref, ge_ref, gk_ref, gp_ref, gf_ref,
           x32, xb, g32, pc, film, pre, sc, sec, prec, secb, precb, proj, F, S1, M, fc, gpt):
    film[...] = jnp.dot(e_ref[...], fw_ref[...], preferred_element_type=f32)
    gk_ref[...] = jnp.zeros_like(gk_ref)
    ge_ref[...] = jnp.zeros_like(ge_ref)
    gpt[...] = jnp.zeros_like(gpt)

    def tile(ft, carry):
        for f in range(TILE):
            for l in range(2):
                x32[l, pl.ds(f, CELLS, stride=TILE), :] = x_ref[ft * TILE + f, :, l * 128:l * 128 + 128].astype(f32)
            for l in range(3):
                g32[l, pl.ds(f, CELLS, stride=TILE), :] = g_ref[ft * TILE + f, :, l * 128:l * 128 + 128].astype(f32)
        for l in range(2):
            xb[:, l * 128:l * 128 + 128] = x32[l].astype(bf16)
        fm = film[pl.ds(pl.multiple_of(ft * TILE, TILE), TILE), :]
        scale, shift = 1.0 + fm[:, :COUT], fm[:, COUT:]
        for l in range(3):
            sl = slice(l * 128, l * 128 + 128)
            pc[:, sl] = (g32[l].reshape(CELLS, TILE, 128) * scale[None, :, sl]).reshape(ROWS, 128).astype(bf16)
        pre[...] = jnp.dot(xb[...], we_ref[...], preferred_element_type=f32)
        sc[...] = jnp.dot(pc[...], wpt_ref[...], preferred_element_type=f32)

        def lanes(lt, carry):
            vpu_block(pl.multiple_of(lt * 128, 128), pre, sc, dw_ref, F, S1, M, sec, prec, gk_ref)
            return carry
        lax.fori_loop(0, HP // 128, lanes, 0)
        secb[...] = sec[...].astype(bf16)
        precb[...] = prec[...].astype(bf16)
        pj = jnp.dot(secb[...], wp_ref[...], preferred_element_type=f32)
        fr = pl.ds(pl.multiple_of(ft * TILE, TILE), TILE)
        for l in range(3):
            sl = slice(l * 128, l * 128 + 128)
            g3, pj3 = g32[l].reshape(CELLS, TILE, 128), pj[:, sl].reshape(CELLS, TILE, 128)
            fc[fr, sl] = jnp.sum(g3 * pj3, axis=0)
            fc[fr, COUT + l * 128:COUT + l * 128 + 128] = jnp.sum(g3, axis=0)
            proj[l] = (pj3 * scale[None, :, sl] + shift[None, :, sl]).reshape(ROWS, 128)
        for f in range(TILE):
            for l in range(3):
                tok_ref[ft * TILE + f, :, l * 128:l * 128 + 128] = proj[l, pl.ds(f, CELLS, stride=TILE), :].astype(bf16)
        tn = (((0,), (0,)), ((), ()))
        ge_ref[...] += lax.dot_general(xb[...], precb[...], tn, preferred_element_type=f32)
        gpt[...] += lax.dot_general(pc[...], secb[...], tn, preferred_element_type=f32)
        return carry
    lax.fori_loop(0, NT, tile, 0)
    gp_ref[...] = gpt[...].T
    gf_ref[...] = lax.dot_general(e_ref[...], fc[...].astype(bf16), (((0,), (0,)), ((), ())), preferred_element_type=f32)


def compute(frames, emb, g, w_expand, dw_kernel, w_project, film_weight):
    x = jnp.pad(frames, ((0, 4), (0, 0), (0, 24)))
    e = jnp.pad(emb, ((0, 4), (0, 0)))
    gg = jnp.pad(g, ((0, 4), (0, 0), (0, 0)))
    we = jnp.pad(w_expand * jnp.asarray(0.5, bf16), ((0, 24), (0, 16)))
    wp = jnp.pad(w_project, ((0, 16), (0, 0)))
    wpt = jnp.pad((w_project * jnp.asarray(0.5, bf16)).T, ((0, 0), (0, 16)))
    dw = jnp.repeat(jnp.pad(dw_kernel * 0.5, ((0, 0), (0, 16))), 8, axis=0)
    V = pl.BlockSpec(memory_space=pltpu.VMEM)
    S = lambda r, c, t=f32: pltpu.VMEM((r, c), t)
    tok, ge, gk, gp, gf = pl.pallas_call(
        kernel,
        out_shape=(jax.ShapeDtypeStruct((40, CELLS, COUT), bf16), jax.ShapeDtypeStruct((256, HP), f32),
                   jax.ShapeDtypeStruct((72, HP), f32), jax.ShapeDtypeStruct((HP, COUT), f32),
                   jax.ShapeDtypeStruct((EMB, 2 * COUT), f32)),
        in_specs=[V] * 8, out_specs=(V,) * 5,
        scratch_shapes=[pltpu.VMEM((2, ROWS, 128), f32), S(ROWS, 256, bf16), pltpu.VMEM((3, ROWS, 128), f32), S(ROWS, COUT, bf16), S(40, 2 * COUT),
                        S(ROWS, HP), S(ROWS, HP), S(ROWS, HP), S(ROWS, HP), S(ROWS, HP, bf16), S(ROWS, HP, bf16), pltpu.VMEM((3, ROWS, 128), f32),
                        S(ROWS, 128), S(ROWS, 128), S(ROWS, 128), S(40, 2 * COUT), S(COUT, HP)],
        compiler_params=pltpu.CompilerParams(vmem_limit_bytes=60 * 2**20),
    )(x, e, gg, we, dw, wp, wpt, film_weight)
    gk = gk.reshape(9, 8, HP).sum(axis=1)[:, :HID]
    return tok[:FR], ge[:CIN, :HID], gk, gp[:HID], gf


def per_device(
    replay,
    instructions,
    owners,
    episode_rows,
    frame_steps,
    w_expand,
    dw_kernel,
    w_project,
    film_weight,
    token_grad,
):
    peer_count = lax.axis_size("dp")
    frame_count = owners.shape[0]
    capacity = max(2, (2 * frame_count + peer_count - 1) // peer_count)
    slot_count = peer_count * capacity
    episode_length = replay.shape[1]
    cell_count = replay.shape[2]
    out_width = w_project.shape[1]
    owner_ids = owners[:, 0]
    positions = jnp.arange(frame_count, dtype=jnp.int32)
    earlier = (owner_ids[:, None] == owner_ids[None, :]) & (positions[:, None] < positions[None, :])
    rank_within = jnp.sum(earlier.astype(jnp.int32), axis=0)
    target = owner_ids * capacity + rank_within
    onehot = target[:, None] == jnp.arange(slot_count, dtype=jnp.int32)[None, :]
    wanted = episode_rows * episode_length + frame_steps
    request = jnp.sum(jnp.where(onehot, wanted[:, None], 0), axis=0).reshape(peer_count, capacity)
    asked_rows = lax.all_to_all(request, "dp", split_axis=0, concat_axis=0, tiled=True).reshape(
        slot_count
    )
    stored = replay.reshape(-1, cell_count, replay.shape[3])
    picked = jnp.take(stored, asked_rows, axis=0)
    picked_embedding = jnp.take(instructions, asked_rows // episode_length, axis=0)
    arrived, arrived_embedding = (
        lax.all_to_all(
            picked.reshape(peer_count, capacity, cell_count, -1),
            "dp",
            split_axis=0,
            concat_axis=0,
            tiled=True,
        ),
        lax.all_to_all(
            picked_embedding.reshape(peer_count, capacity, -1),
            "dp",
            split_axis=0,
            concat_axis=0,
            tiled=True,
        ),
    )
    frames = jnp.take(arrived.reshape(slot_count, cell_count, -1), target, axis=0)
    embedding = jnp.take(arrived_embedding.reshape(slot_count, -1), target, axis=0)
    cotangent = token_grad.reshape(frame_count, cell_count, out_width)
    tokens, *gradients = compute(
        frames, embedding, cotangent, w_expand, dw_kernel, w_project, film_weight
    )
    tokens_out = tokens.reshape(token_grad.shape)
    summed = lax.psum(tuple(gradients), ("dp", "replica"))
    return (tokens_out, summed[0], summed[1], summed[2], summed[3])


def solution(mesh):
    in_specs = (
        P(("dp", "replica"), None, None, None),
        P(("dp", "replica"), None),
        P(("dp", "replica"), None),
        P(("dp", "replica")),
        P(("dp", "replica")),
        P(),
        P(),
        P(),
        P(),
        P(("dp", "replica"), None, None, None),
    )
    out_specs = (P(("dp", "replica"), None, None, None), P(), P(), P(), P())
    return jax.shard_map(
        per_device, mesh=mesh, in_specs=in_specs, out_specs=out_specs, check_vma=False
    )
```

time: 1080 us -> 375 us (0.35)
  other arithmetic: 316 us -> 9.04 us
  local copies, waits for them, and re-layouts: 316 us -> 55.6 us
  matrix products: 187 us -> 0 us
  Pallas kernels: 0 us -> 74.1 us
  waiting for transfers between devices: 142 us -> 128 us
    dot_general x48 -> x0, matrix products: 187 us -> none  [the longest x6 75.3 us: backward(): lax.dot_general(proj_cot, w_project, (((1,), (1,)), ((), ())), preferred_...]
    convert_element_type x30 -> x0, other arithmetic: 154 us -> none  [the longest x6 128 us: backward(): pre_cot = (first_cot.reshape(amount * cell_count, -1) * first_slope.resha...]
    mul x6 -> x2, other arithmetic: 138 us -> 0.08 us  [the longest x1 0.07 us: compute(): we = jnp.pad(w_expand * jnp.asarray(0.5, bf16), ((0, 24), (0, 16)))]
    dynamic_slice x48 -> x0, local copies, waits for them, and re-layouts: 80.4 us -> none  [the longest x36 68.8 us: backward_blocks(): lax.scan(backward_one_block, start_totals, (regroup(frames), regroup(embe...]
    pallas_call x0 -> x1, Pallas kernels: none -> 74.1 us  [compute(): pl.pallas_call(kernel, out_shape=(jax.ShapeDtypeStruct((40, CELLS, COUT),...]
    dynamic_update_slice x24 -> x0, local copies, waits for them, and re-layouts: 51.6 us -> none  [forward_blocks(): lax.map(forward_one_block, (frames.reshape(groups, stride, cell_count, in...]
    reshape x36 -> x1, local copies, waits for them, and re-layouts: 34.6 us -> 0.8 us  [compute(): dw = jnp.repeat(jnp.pad(dw_kernel * 0.5, ((0, 0), (0, 16))), 8, axis=0)]
    broadcast_in_dim x13 -> x0, local copies, waits for them, and re-layouts: 31.4 us -> none  [the longest x12 31.3 us: forward_blocks(): lax.map(forward_one_block, (frames.reshape(groups, stride, cell_count, in...]
  transfers between devices with their start and end apart: 4 -> 4, of which waited for: 2 -> 2; matrix products, arithmetic and copies ran while one was open for 3% -> 11% of each run, Pallas kernels for 0% -> 0%
where the time goes in v1:
time: 375 us; the launch traced here: 374 us
  waiting for transfers between devices  128 us (34%)
  Pallas kernels  74.1 us (20%)
  blocking collectives  68.3 us (18%)
  local copies, waits for them, and re-layouts  55.6 us (15%)
  starting transfers between devices  24.8 us (7%)
  between operations  14.2 us (4%)
  other arithmetic  9.04 us (2%)
    psum x1, waiting for transfers between devices, per_device(): summed = lax.psum(tuple(gradients), ('dp', 'replica'))  85.4 us
    pallas_call x1, Pallas kernels, compute(): pl.pallas_call(kernel, out_shape=(jax.ShapeDtypeStruct((40, CELLS, COUT),...  74.1 us
    psum x1, blocking collectives, per_device(): summed = lax.psum(tuple(gradients), ('dp', 'replica'))  68.3 us
    all_to_all x1, waiting for transfers between devices, per_device(): lax.all_to_all(picked.reshape(peer_count, capacity, cell_count, -1), 'dp'...  43 us
    unnamed x27, local copies, waits for them, and re-layouts  16.4 us
    reshape x1, local copies, waits for them, and re-layouts, per_device(): stored = replay.reshape(-1, cell_count, replay.shape[3])  11.2 us
    all_to_all x1, starting transfers between devices, per_device(): lax.all_to_all(request, 'dp', split_axis=0, concat_axis=0, tiled=True)  9.6 us
    all_to_all x1, starting transfers between devices, per_device(): lax.all_to_all(picked.reshape(peer_count, capacity, cell_count, -1), 'dp'...  7.56 us
  transfers between devices with their start and end apart: 4, of which 2 were waited for; matrix products, arithmetic and copies ran while one was open for 11% of the time, Pallas kernels for 0%

profile of v1, /device:TPU:1, one launch (start us, length us, event | category | flops | bytes accessed | tf_op | source)
XLA Modules:
  0.0 374.4 jit_solution(5839025709561184896)
XLA Ops:
  7.2 0.8 convert_reduce_fusion
  9.4 0.7 all_to_all.12
  10.1 9.6 %all-to-all-start = ((s32[32,1,3]{2,1,0:T(1,128)}), s32[32,1,3]{2,1,0:T(1,128)S(1)}, u32[]{:S(2)}, u32[]{:S(2)}) async-start(s32[32,1,3]{2,1,0:T(1,128)} %bitcast.4), calls=%async_computation | async-start | bytes 32768 | tf_op jit(solution)/shard_map/all_to_all | solution.py:177
  19.8 7.4 %copy.47 = bf16[8,24,81,232]{3,1,0,2:T(8,128)(2,1)} copy(bf16[8,24,81,232]{3,1,2,0:T(8,128)(2,1)} %param.10) | data formatting | bytes 14432256 | tf_op args[0]
  27.2 11.2 %copy.48 = bf16[192,81,232]{2,1,0:T(8,128)(2,1)} copy(bf16[192,81,232]{2,0,1:T(8,128)(2,1)} %bitcast.53) | data formatting | bytes 14432256 | tf_op jit(solution)/shard_map/reshape | solution.py:180
  38.9 0.7 reduce.3
  39.9 0.8 gather_fusion.2
  40.9 0.8 broadcast_select_fusion.2
  41.7 7.4 %all-to-all-start.2 = ((bf16[32,3,512]{2,1,0:T(4,128)(2,1)}), bf16[32,3,512]{2,1,0:T(4,128)(2,1)S(1)}, u32[]{:S(2)}, u32[]{:S(2)}) async-start(bf16[32,3,512]{2,1,0:T(4,128)(2,1)} %broadcast_select_fusion.2), calls=%async_computation.2 | async-start | bytes 262144 | tf_op jit(solution)/shard_map/all_to_all | solution.py:191
  49.1 6.5 %gather_fusion = bf16[96,81,232]{2,1,0:T(8,128)(2,1)} fusion(bf16[192,81,232]{2,1,0:T(8,128)(2,1)} %copy.48, s32[1024]{0:T(1024)S(1)} %get-tuple-element.25), kind=kCustom, calls=%fused_computation | custom fusion | bytes 7216512 | tf_op jit(solution)/shard_map/jit(_take)/gather | solution.py:181
  55.6 4.7 %broadcast_select_fusion = bf16[32,3,81,232]{3,2,1,0:T(8,128)(2,1)} fusion(bf16[32,3,81,232]{3,2,1,0:T(8,128)(2,1)} %bitcast.54, pred[32,3]{1,0:T(8,128)(4,1)S(1)} %copy.46), kind=kLoop, calls=%fused_computation.4 | loop fusion | flops 1804032 | bytes 7216224 | tf_op jit(solution)/shard_map/jit(_take)/select_n | solution.py:181
  60.3 7.6 %all-to-all-start.1 = ((bf16[32,3,81,232]{3,2,1,0:T(8,128)(2,1)}), bf16[32,3,81,232]{3,2,1,0:T(8,128)(2,1)}, u32[]{:S(2)}, u32[]{:S(2)}) async-start(bf16[32,3,81,232]{3,2,1,0:T(8,128)(2,1)} %broadcast_select_fusion), calls=%async_computation.1 | async-start | bytes 8650752 | tf_op jit(solution)/shard_map/all_to_all | solution.py:184
  68.1 1.3 copy.50
  69.3 1.1 pad.33.wp_ref
  70.4 3.6 pad.30.g_ref
  74.1 0.9 pad.31.we_ref
  75.2 1.1 pad.34.wpt_ref
  76.3 0.8 broadcast_bitcast_fusion.dw_ref
  78.6 43.0 %all-to-all-done.1 = bf16[32,3,81,232]{3,2,1,0:T(8,128)(2,1)} async-done(((bf16[32,3,81,232]{3,2,1,0:T(8,128)(2,1)}), bf16[32,3,81,232]{3,2,1,0:T(8,128)(2,1)}, u32[]{:S(2)}, u32[]{:S(2)}) %all-to-all-start.1) | async-done | bytes 3608096 | tf_op jit(solution)/shard_map/all_to_all | solution.py:184
  121.6 2.9 gather_fusion.1
  124.7 1.5 pad.28.x_ref
  126.2 74.1 %shard_map.137 = (bf16[40,81,384]{2,1,0:T(8,128)(2,1)}, f32[256,1408]{1,0:T(8,128)}, f32[72,1408]{1,0:T(8,128)}, f32[1408,384]{1,0:T(8,128)}, f32[512,768]{1,0:T(8,128)}) custom-call(bf16[40,81,256]{2,1,0:T(8,128)(2,1)} %pad.28.x_ref, bf16[40,512]{1,0:T(8,128)(2,1)} %pad.29.e_ref, bf16[40,81,384]{2,1,0:T(8,128)(2,1)} %pad.30.g_ref, ...), custom_call_target="tpu_custom_call" | custom-call | tf_op jit(solution)/shard_map/pallas_call | solution.py:135
  200.3 2.6 slice.13
  202.9 1.5 slice.15
  204.4 1.7 copy-done.3
  206.1 1.7 slice.12
  207.9 68.3 %psum.29 = f32[9,1392]{1,0:T(8,128)} all-reduce(f32[9,1392]{1,0:T(8,128)S(1)} %bitcast.57), channel_id=1, replica_groups=mesh['dp'=32,'replica'=4] {'dp','replica'}, use_global_device_ids=true, to_apply=%region_4.5 | all-reduce | flops 12528 | bytes 100224 | tf_op jit(solution)/shard_map/psum | solution.py:206
  276.2 85.4 %all-reduce.10.cloned.1.call-done = (f32[232,1392]{1,0:T(8,128)}, f32[1392,384]{1,0:T(8,128)}, f32[512,768]{1,0:T(8,128)}) async-done(((f32[232,1392]{1,0:T(8,128)}, f32[1392,384]{1,0:T(8,128)}, f32[512,768]{1,0:T(8,128)}), (f32[232,1392]{1,0:T(8,128)}, f32[1392,384]{1,0:T(8,128)}, f32[512,768]{1,0:T(8,128)})) %all-reduce.10.cloned.1.call-update) | async-done | bytes 5002768 | tf_op jit(solution)/shard_map/psum | solution.py:206
  361.6 2.6 copy.55
  364.2 1.3 copy.56
  365.5 0.8 copy-done.6
  366.4 1.1 copy.57
  (48 shorter events, 4.7 us)
Async XLA Ops:
  7.2 32.8 %copy-start = (bf16[8,512]{1,0:T(8,128)(2,1)S(1)}, bf16[8,512]{1,0:T(8,128)(2,1)}, u32[]{:S(2)}) copy-start(bf16[8,512]{1,0:T(8,128)(2,1)} %param.11) | copy-start | bytes 24580
  10.1 28.2 %all-to-all-start = ((s32[32,1,3]{2,1,0:T(1,128)}), s32[32,1,3]{2,1,0:T(1,128)S(1)}, u32[]{:S(2)}, u32[]{:S(2)}) async-start(s32[32,1,3]{2,1,0:T(1,128)} %bitcast.4), calls=%async_computation | async-start | bytes 32768 | tf_op jit(solution)/shard_map/all_to_all | solution.py:177
  41.7 18.6 %all-to-all-start.2 = ((bf16[32,3,512]{2,1,0:T(4,128)(2,1)}), bf16[32,3,512]{2,1,0:T(4,128)(2,1)S(1)}, u32[]{:S(2)}, u32[]{:S(2)}) async-start(bf16[32,3,512]{2,1,0:T(4,128)(2,1)} %broadcast_select_fusion.2), calls=%async_computation.2 | async-start | bytes 262144 | tf_op jit(solution)/shard_map/all_to_all | solution.py:191
  60.2 7.8 %copy-start.2 = (bf16[1392,384]{1,0:T(8,128)(2,1)S(1)}, bf16[1392,384]{1,0:T(8,128)(2,1)}, u32[]{:S(2)}) copy-start(bf16[1392,384]{1,0:T(8,128)(2,1)} %param.17) | copy-start | bytes 3207172
  60.3 61.4 %all-to-all-start.1 = ((bf16[32,3,81,232]{3,2,1,0:T(8,128)(2,1)}), bf16[32,3,81,232]{3,2,1,0:T(8,128)(2,1)}, u32[]{:S(2)}, u32[]{:S(2)}) async-start(bf16[32,3,81,232]{3,2,1,0:T(8,128)(2,1)} %broadcast_select_fusion), calls=%async_computation.1 | async-start | bytes 8650752 | tf_op jit(solution)/shard_map/all_to_all | solution.py:184
  67.8 293.8 %all-reduce.10.cloned.1.call-start = ((), (), s32[]{:S(2)}) async-start(), calls=%async_computation.3 | async-start | bytes 10035200 | tf_op jit(solution)/shard_map/psum | solution.py:206
  70.4 3.6 copy-start.7
  75.1 1.2 copy-start.9
  75.2 1.1 copy-start.10
  200.3 2.6 copy-start.5
  204.4 1.8 copy-start.3
  206.1 1.7 copy-start.8
  361.6 2.6 copy-start.4
  364.2 2.2 copy-start.6
  364.2 3.3 copy-start.1
Sparse Core Ops, SparseCore 0:
  204.5 157.0 all-reduce.9

commit v2 on v1

--- a/solution.py
+++ b/solution.py
@@ -8,6 +8,8 @@
 CIN, HID, COUT, EMB, FR = 232, 1392, 384, 512, 36
 HP = 1408
 NT = 5
+GR = 10240
+GE, GK, GP, GF = 0, 2640, 2816, 6992
 ROWS = CELLS * TILE
 f32, bf16 = jnp.float32, jnp.bfloat16
 
@@ -73,19 +75,22 @@
 
 
 def kernel(x_ref, e_ref, g_ref, we_ref, dw_ref, wp_ref, wpt_ref, fw_ref,
-           tok_ref, ge_ref, gk_ref, gp_ref, gf_ref,
-           x32, xb, g32, pc, film, pre, sc, sec, prec, secb, precb, proj, F, S1, M, fc, gpt):
-    film[...] = jnp.dot(e_ref[...], fw_ref[...], preferred_element_type=f32)
+           tok_ref, sum_ref,
+           x32, xb, g32, pc, film, pre, sc, sec, prec, secb, precb, proj, F, S1, M, fc, gpt, ge_ref, gk_ref):
+    film[FR:, :] = jnp.zeros((NT * TILE - FR, 2 * COUT), f32)
+    film[:FR, :] = jnp.dot(e_ref[...], fw_ref[...], preferred_element_type=f32)
     gk_ref[...] = jnp.zeros_like(gk_ref)
     ge_ref[...] = jnp.zeros_like(ge_ref)
     gpt[...] = jnp.zeros_like(gpt)
 
     def tile(ft, carry):
         for f in range(TILE):
+            j = ft * TILE + f
+            held, keep = jnp.minimum(j, FR - 1), jnp.where(j < FR, 1.0, 0.0)
             for l in range(2):
-                x32[l, pl.ds(f, CELLS, stride=TILE), :] = x_ref[ft * TILE + f, :, l * 128:l * 128 + 128].astype(f32)
+                x32[l, pl.ds(f, CELLS, stride=TILE), :] = x_ref[held, :, l * 128:l * 128 + 128].astype(f32) * keep
             for l in range(3):
-                g32[l, pl.ds(f, CELLS, stride=TILE), :] = g_ref[ft * TILE + f, :, l * 128:l * 128 + 128].astype(f32)
+                g32[l, pl.ds(f, CELLS, stride=TILE), :] = g_ref[held, :, l * 128:l * 128 + 128].astype(f32) * keep
         for l in range(2):
             xb[:, l * 128:l * 128 + 128] = x32[l].astype(bf16)
         fm = film[pl.ds(pl.multiple_of(ft * TILE, TILE), TILE), :]
@@ -111,40 +116,176 @@
             fc[fr, COUT + l * 128:COUT + l * 128 + 128] = jnp.sum(g3, axis=0)
             proj[l] = (pj3 * scale[None, :, sl] + shift[None, :, sl]).reshape(ROWS, 128)
         for f in range(TILE):
-            for l in range(3):
-                tok_ref[ft * TILE + f, :, l * 128:l * 128 + 128] = proj[l, pl.ds(f, CELLS, stride=TILE), :].astype(bf16)
+            @pl.when(ft * TILE + f < FR)
+            def _(f=f):
+                for l in range(3):
+                    tok_ref[ft * TILE + f, :, l * 128:l * 128 + 128] = proj[l, pl.ds(f, CELLS, stride=TILE), :].astype(bf16)
         tn = (((0,), (0,)), ((), ()))
         ge_ref[...] += lax.dot_general(xb[...], precb[...], tn, preferred_element_type=f32)
         gpt[...] += lax.dot_general(pc[...], secb[...], tn, preferred_element_type=f32)
         return carry
     lax.fori_loop(0, NT, tile, 0)
-    gp_ref[...] = gpt[...].T
-    gf_ref[...] = lax.dot_general(e_ref[...], fc[...].astype(bf16), (((0,), (0,)), ((), ())), preferred_element_type=f32)
+    gk = jnp.concatenate([jnp.sum(gk_ref[...].reshape(9, 8, HP), axis=1), jnp.zeros((7, HP), f32)], axis=0).astype(bf16)
+    for lt in range(HP // 128):
+        ln = slice(lt * 128, lt * 128 + 128)
+        sum_ref[GE + lt * 240:GE + lt * 240 + 240, :] = ge_ref[:240, ln].astype(bf16)
+        sum_ref[GK + lt * 16:GK + lt * 16 + 16, :] = gk[:, ln]
+    for l in range(3):
+        sum_ref[GP + l * HID:GP + l * HID + HID, :] = gpt[l * 128:l * 128 + 128, :].T[:HID].astype(bf16)
+    gf = lax.dot_general(e_ref[...], fc[:FR, :].astype(bf16), (((0,), (0,)), ((), ())), preferred_element_type=f32).astype(bf16)
+    for l in range(6):
+        sum_ref[GF + l * EMB:GF + l * EMB + EMB, :] = gf[:, l * 128:l * 128 + 128]
+    sum_ref[GF + 6 * EMB:, :] = jnp.zeros((GR - GF - 6 * EMB, 128), bf16)
 
 
 def compute(frames, emb, g, w_expand, dw_kernel, w_project, film_weight):
-    x = jnp.pad(frames, ((0, 4), (0, 0), (0, 24)))
-    e = jnp.pad(emb, ((0, 4), (0, 0)))
-    gg = jnp.pad(g, ((0, 4), (0, 0), (0, 0)))
+    x = jnp.pad(frames, ((0, 0), (0, 0), (0, 24)))
     we = jnp.pad(w_expand * jnp.asarray(0.5, bf16), ((0, 24), (0, 16)))
     wp = jnp.pad(w_project, ((0, 16), (0, 0)))
     wpt = jnp.pad((w_project * jnp.asarray(0.5, bf16)).T, ((0, 0), (0, 16)))
     dw = jnp.repeat(jnp.pad(dw_kernel * 0.5, ((0, 0), (0, 16))), 8, axis=0)
     V = pl.BlockSpec(memory_space=pltpu.VMEM)
     S = lambda r, c, t=f32: pltpu.VMEM((r, c), t)
-    tok, ge, gk, gp, gf = pl.pallas_call(
+    return pl.pallas_call(
         kernel,
-        out_shape=(jax.ShapeDtypeStruct((40, CELLS, COUT), bf16), jax.ShapeDtypeStruct((256, HP), f32),
-                   jax.ShapeDtypeStruct((72, HP), f32), jax.ShapeDtypeStruct((HP, COUT), f32),
-                   jax.ShapeDtypeStruct((EMB, 2 * COUT), f32)),
-        in_specs=[V] * 8, out_specs=(V,) * 5,
-        scratch_shapes=[pltpu.VMEM((2, ROWS, 128), f32), S(ROWS, 256, bf16), pltpu.VMEM((3, ROWS, 128), f32), S(ROWS, COUT, bf16), S(40, 2 * COUT),
+        out_shape=(jax.ShapeDtypeStruct((FR, CELLS, COUT), bf16), jax.ShapeDtypeStruct((GR, 128), bf16)),
+        in_specs=[V] * 8, out_specs=(V,) * 2,
+        scratch_shapes=[pltpu.VMEM((2, ROWS, 128), f32), S(ROWS, 256, bf16), pltpu.VMEM((3, ROWS, 128), f32), S(ROWS, COUT, bf16), S(NT * TILE, 2 * COUT),
                         S(ROWS, HP), S(ROWS, HP), S(ROWS, HP), S(ROWS, HP), S(ROWS, HP, bf16), S(ROWS, HP, bf16), pltpu.VMEM((3, ROWS, 128), f32),
-                        S(ROWS, 128), S(ROWS, 128), S(ROWS, 128), S(40, 2 * COUT), S(COUT, HP)],
+                        S(ROWS, 128), S(ROWS, 128), S(ROWS, 128), S(NT * TILE, 2 * COUT), S(COUT, HP), S(256, HP), S(72, HP)],
         compiler_params=pltpu.CompilerParams(vmem_limit_bytes=60 * 2**20),
-    )(x, e, gg, we, dw, wp, wpt, film_weight)
-    gk = gk.reshape(9, 8, HP).sum(axis=1)[:, :HID]
-    return tok[:FR], ge[:CIN, :HID], gk, gp[:HID], gf
+        name="film_block",
+    )(x, emb, g, we, dw, wp, wpt, film_weight)
+
+
+PIECES = (32, 32, 16)
+STARTS = (0, 4096, 8192)
+ORDERS = (("x", "y", "z"), ("y", "z", "x"), ("z", "x", "y"))
+
+
+def place():
+    dp, rep = lax.axis_index("dp"), lax.axis_index("replica")
+    return {"x": rep, "y": dp // 8, "z": (dp // 2) % 4, "core": dp % 2}
+
+
+def device_of(at):
+    return ((at["y"] * 4 + at["z"]) * 2 + at["core"], at["x"])
+
+
+def shifted(at, axis, d):
+    size = 2 if axis == "core" else 4
+    other = dict(at)
+    other[axis] = (at[axis] + d) % size
+    return other
+
+
+def reduce_kernel(g_ref, ge_ref, gk_ref, gp_ref, gf_ref, total, part, r0, r1, r2, r3, send, recv):
+    at = place()
+    barrier = pltpu.get_barrier_semaphore()
+    peers = [shifted(at, "core", 1)] + [shifted(at, a, d) for a in "xyz" for d in (1, 2, 3)]
+    for p in peers:
+        pl.semaphore_signal(barrier, inc=1, device_id=device_of(p), device_id_type=pl.DeviceIdType.MESH)
+    pl.semaphore_wait(barrier, len(peers))
+    land = (r0, r1, r2, r3)
+    waits = []
+
+    def push(src, dst, stage, s, d, peer):
+        copy = pltpu.make_async_remote_copy(src_ref=src, dst_ref=dst, send_sem=send.at[stage, s, d], recv_sem=recv.at[stage, s, d],
+                                            device_id=device_of(peer), device_id_type=pl.DeviceIdType.MESH)
+        copy.start()
+        waits.append(copy)
+        return copy
+
+    def span(base, index, rows):
+        return pl.ds(pl.multiple_of(base + index * rows, 16), rows)
+
+    state = []
+    for s, r in enumerate(PIECES):
+        base, half = STARTS[s], 64 * r
+        peer = shifted(at, "core", 1)
+        c = push(g_ref.at[span(base, peer["core"], half)], r0.at[pl.ds(base // 2, half)], 0, s, 0, peer)
+        state.append([c])
+    for stage in (1, 2, 3):
+        for s, r in enumerate(PIECES):
+            axis = ORDERS[s][stage - 1]
+            have = r * 4 ** (4 - stage)
+            base = STARTS[s] // 2
+            for c in state[s]:
+                c.wait_recv()
+            if stage == 1:
+                mine = g_ref[span(STARTS[s], at["core"], have)].astype(f32) + r0[pl.ds(base, have)].astype(f32)
+            else:
+                prev = land[stage - 1]
+                pb = base // 4 ** (stage - 1)
+                old = part[stage - 2, span(base, at[ORDERS[s][stage - 2]], have)].astype(f32)
+                mine = old
+                for d in (1, 2, 3):
+                    mine = mine + prev[d - 1, pl.ds(pb, have)].astype(f32)
+            part[stage - 1, pl.ds(base, have)] = mine.astype(bf16)
+            block = have // 4
+            state[s] = []
+            for d in (1, 2, 3):
+                peer = shifted(at, axis, d)
+                state[s].append(push(part.at[stage - 1, span(base, peer[axis], block)],
+                                     land[stage].at[d - 1, pl.ds(base // 4 ** stage, block)], stage, s, d - 1, peer))
+    where = []
+    for s, r in enumerate(PIECES):
+        for c in state[s]:
+            c.wait_recv()
+        base = STARTS[s] // 2
+        mine = part[2, span(base, at[ORDERS[s][2]], r)].astype(f32)
+        for d in (1, 2, 3):
+            mine = mine + r3[d - 1, pl.ds(base // 64, r)].astype(f32)
+        a1, a2, a3 = ORDERS[s]
+        index = ((at["core"] * 4 + at[a1]) * 4 + at[a2]) * 4 + at[a3]
+        where.append(index)
+        total[span(STARTS[s], index, r)] = mine.astype(bf16)
+        state[s] = []
+        for d in (1, 2, 3):
+            sl = span(STARTS[s], index, r)
+            state[s].append(push(total.at[sl], total.at[sl], 4, s, d - 1, shifted(at, a3, d)))
+    for stage in (5, 6, 7):
+        for s, r in enumerate(PIECES):
+            for c in state[s]:
+                c.wait_recv()
+            rows = r * 4 ** (stage - 4)
+            index = where[s] // 4 ** (stage - 4)
+            sl = span(STARTS[s], index, rows)
+            state[s] = []
+            if stage == 7:
+                state[s].append(push(total.at[sl], total.at[sl], stage, s, 0, shifted(at, "core", 1)))
+            else:
+                axis = ORDERS[s][6 - stage]
+                for d in (1, 2, 3):
+                    state[s].append(push(total.at[sl], total.at[sl], stage, s, d - 1, shifted(at, axis, d)))
+    for s in range(3):
+        for c in state[s]:
+            c.wait_recv()
+    for c in waits:
+        c.wait_send()
+    for lt in range(11):
+        w = min(128, HID - lt * 128)
+        ge_ref[:, lt * 128:lt * 128 + w] = total[GE + lt * 240:GE + lt * 240 + 240].astype(f32)[:CIN, :w]
+        gk_ref[:, lt * 128:lt * 128 + w] = total[GK + lt * 16:GK + lt * 16 + 16].astype(f32)[:9, :w]
+    for l in range(3):
+        gp_ref[:, l * 128:l * 128 + 128] = total[GP + l * HID:GP + l * HID + HID].astype(f32)
+    for l in range(6):
+        gf_ref[:, l * 128:l * 128 + 128] = total[GF + l * EMB:GF + l * EMB + EMB].astype(f32)
+
+
+def all_reduce(g):
+    V = pl.BlockSpec(memory_space=pltpu.VMEM)
+    return pl.pallas_call(
+        reduce_kernel,
+        out_shape=(jax.ShapeDtypeStruct((CIN, HID), f32), jax.ShapeDtypeStruct((9, HID), f32),
+                   jax.ShapeDtypeStruct((HID, COUT), f32), jax.ShapeDtypeStruct((EMB, 2 * COUT), f32)),
+        in_specs=[V], out_specs=(V,) * 4,
+        scratch_shapes=[pltpu.VMEM((GR, 128), bf16), pltpu.VMEM((3, GR // 2, 128), bf16), pltpu.VMEM((GR // 2, 128), bf16),
+                        pltpu.VMEM((3, GR // 8, 128), bf16), pltpu.VMEM((3, GR // 32, 128), bf16), pltpu.VMEM((3, GR // 128, 128), bf16),
+                        pltpu.SemaphoreType.DMA((8, 3, 3)), pltpu.SemaphoreType.DMA((8, 3, 3))],
+        compiler_params=pltpu.CompilerParams(vmem_limit_bytes=48 * 2**20, collective_id=1, has_side_effects=True),
+        name="grad_sum",
+    )(g)
 
 
 def per_device(
@@ -199,11 +340,11 @@
     frames = jnp.take(arrived.reshape(slot_count, cell_count, -1), target, axis=0)
     embedding = jnp.take(arrived_embedding.reshape(slot_count, -1), target, axis=0)
     cotangent = token_grad.reshape(frame_count, cell_count, out_width)
-    tokens, *gradients = compute(
+    tokens, partial_sums = compute(
         frames, embedding, cotangent, w_expand, dw_kernel, w_project, film_weight
     )
     tokens_out = tokens.reshape(token_grad.shape)
-    summed = lax.psum(tuple(gradients), ("dp", "replica"))
+    summed = all_reduce(partial_sums)
     return (tokens_out, summed[0], summed[1], summed[2], summed[3])
 
 

time: 375 us -> 244 us (0.65)
  waiting for transfers between devices: 128 us -> 46.9 us
  blocking collectives: 68.3 us -> 0 us
  Pallas kernels: 74.1 us -> 120 us
  local copies, waits for them, and re-layouts: 55.6 us -> 42 us
  between operations: 14.2 us -> 0.81 us
    psum x1 -> x0, waiting for transfers between devices: 85.4 us -> none  [per_device(): summed = lax.psum(tuple(gradients), ('dp', 'replica'))]
    psum x1 -> x0, blocking collectives: 68.3 us -> none  [per_device(): summed = lax.psum(tuple(gradients), ('dp', 'replica'))]
    pallas_call x1 -> x2, Pallas kernels: 74.1 us -> 120 us  [the longest x1 75.5 us: compute(): pl.pallas_call(kernel, out_shape=(jax.ShapeDtypeStruct((FR, CELLS, COUT),...]
    slice x3 -> x0, local copies, waits for them, and re-layouts: 5.75 us -> none  [compute(): return (tok[:FR], ge[:CIN, :HID], gk, gp[:HID], gf)]
    pad x3 -> x1, local copies, waits for them, and re-layouts: 5.75 us -> 1.43 us  [compute(): x = jnp.pad(frames, ((0, 0), (0, 0), (0, 24)))]
    all_to_all x1, waiting for transfers between devices: 43 us -> 46.9 us  [per_device(): lax.all_to_all(picked.reshape(peer_count, capacity, cell_count, -1), 'dp'...]
    unnamed x27 -> x18, local copies, waits for them, and re-layouts: 16.4 us -> 12.9 us
  transfers between devices with their start and end apart: 4 -> 3, of which waited for: 2 -> 1; matrix products, arithmetic and copies ran while one was open for 11% -> 15% of each run, Pallas kernels for 0% -> 0%
where the time goes in v2:
time: 244 us
  Pallas kernels  120 us (49%)
  waiting for transfers between devices  46.9 us (19%)
  local copies, waits for them, and re-layouts  42 us (17%)
  starting transfers between devices  24.6 us (10%)
  other arithmetic  9.56 us (4%)
    pallas_call x1, Pallas kernels, compute(): pl.pallas_call(kernel, out_shape=(jax.ShapeDtypeStruct((FR, CELLS, COUT),...  75.5 us
    all_to_all x1, waiting for transfers between devices, per_device(): lax.all_to_all(picked.reshape(peer_count, capacity, cell_count, -1), 'dp'...  46.9 us
    pallas_call x1, Pallas kernels, all_reduce(): pl.pallas_call(reduce_kernel, out_shape=(jax.ShapeDtypeStruct((CIN, HID),...  44.4 us
    unnamed x18, local copies, waits for them, and re-layouts  12.9 us
    reshape x1, local copies, waits for them, and re-layouts, per_device(): stored = replay.reshape(-1, cell_count, replay.shape[3])  11.2 us
    all_to_all x1, starting transfers between devices, per_device(): lax.all_to_all(request, 'dp', split_axis=0, concat_axis=0, tiled=True)  9.6 us
    all_to_all x1, starting transfers between devices, per_device(): lax.all_to_all(picked.reshape(peer_count, capacity, cell_count, -1), 'dp'...  7.57 us
    all_to_all x1, starting transfers between devices, per_device(): lax.all_to_all(picked_embedding.reshape(peer_count, capacity, -1), 'dp',...  7.38 us
  transfers between devices with their start and end apart: 3, of which 1 were waited for; matrix products, arithmetic and copies ran while one was open for 15% of the time, Pallas kernels for 0%

profile of v2, /device:TPU:1, one launch (start us, length us, event | category | flops | bytes accessed | tf_op | source)
XLA Modules:
  0.0 243.8 jit_solution(7191386962594955263)
XLA Ops:
  0.6 0.8 convert_reduce_fusion
  1.5 0.7 fusion.6
  2.1 0.7 multiply_add_fusion
  2.9 0.7 all_to_all.12
  3.6 9.6 %all-to-all-start = ((s32[32,1,3]{2,1,0:T(1,128)}), s32[32,1,3]{2,1,0:T(1,128)S(1)}, u32[]{:S(2)}, u32[]{:S(2)}) async-start(s32[32,1,3]{2,1,0:T(1,128)} %bitcast.4), calls=%async_computation | async-start | bytes 32768 | tf_op jit(solution)/shard_map/all_to_all | solution.py:318
  13.2 7.4 %copy.47 = bf16[8,24,81,232]{3,1,0,2:T(8,128)(2,1)} copy(bf16[8,24,81,232]{3,1,2,0:T(8,128)(2,1)} %param.10) | data formatting | bytes 14432256 | tf_op args[0]
  20.7 11.2 %copy.48 = bf16[192,81,232]{2,1,0:T(8,128)(2,1)} copy(bf16[192,81,232]{2,0,1:T(8,128)(2,1)} %bitcast.50) | data formatting | bytes 14432256 | tf_op jit(solution)/shard_map/reshape | solution.py:321
  31.8 0.5 broadcast.151
  32.4 0.7 reduce.3
  33.4 0.8 gather_fusion.2
  34.3 0.8 broadcast_select_fusion.2
  35.1 7.4 %all-to-all-start.2 = ((bf16[32,3,512]{2,1,0:T(4,128)(2,1)}), bf16[32,3,512]{2,1,0:T(4,128)(2,1)S(1)}, u32[]{:S(2)}, u32[]{:S(2)}) async-start(bf16[32,3,512]{2,1,0:T(4,128)(2,1)} %broadcast_select_fusion.2), calls=%async_computation.2 | async-start | bytes 262144 | tf_op jit(solution)/shard_map/all_to_all | solution.py:332
  42.5 6.5 %gather_fusion = bf16[96,81,232]{2,1,0:T(8,128)(2,1)} fusion(bf16[192,81,232]{2,1,0:T(8,128)(2,1)} %copy.48, s32[1024]{0:T(1024)S(1)} %get-tuple-element.24), kind=kCustom, calls=%fused_computation | custom fusion | bytes 7216512 | tf_op jit(solution)/shard_map/jit(_take)/gather | solution.py:322
  49.0 4.7 %broadcast_select_fusion = bf16[32,3,81,232]{3,2,1,0:T(8,128)(2,1)} fusion(bf16[32,3,81,232]{3,2,1,0:T(8,128)(2,1)} %bitcast.51, pred[32,3]{1,0:T(8,128)(4,1)S(1)} %copy.46), kind=kLoop, calls=%fused_computation.4 | loop fusion | flops 1804032 | bytes 7216224 | tf_op jit(solution)/shard_map/jit(_take)/select_n | solution.py:322
  53.7 7.6 %all-to-all-start.1 = ((bf16[32,3,81,232]{3,2,1,0:T(8,128)(2,1)}), bf16[32,3,81,232]{3,2,1,0:T(8,128)(2,1)}, u32[]{:S(2)}, u32[]{:S(2)}) async-start(bf16[32,3,81,232]{3,2,1,0:T(8,128)(2,1)} %broadcast_select_fusion), calls=%async_computation.1 | async-start | bytes 8650752 | tf_op jit(solution)/shard_map/all_to_all | solution.py:325
  61.3 1.3 copy.50
  62.6 1.1 pad.23.wp_ref
  63.8 1.0 pad.21.we_ref
  64.9 1.1 pad.24.wpt_ref
  66.0 0.8 broadcast_bitcast_fusion.dw_ref
  66.9 0.6 gather_fusion.3
  67.5 0.7 broadcast_select_fusion.3.e_ref
  68.2 46.9 %all-to-all-done.1 = bf16[32,3,81,232]{3,2,1,0:T(8,128)(2,1)} async-done(((bf16[32,3,81,232]{3,2,1,0:T(8,128)(2,1)}), bf16[32,3,81,232]{3,2,1,0:T(8,128)(2,1)}, u32[]{:S(2)}, u32[]{:S(2)}) %all-to-all-start.1) | async-done | bytes 3608096 | tf_op jit(solution)/shard_map/all_to_all | solution.py:325
  115.1 2.9 %gather_fusion.1 = bf16[36,81,232]{2,1,0:T(8,128)(2,1)S(1)} fusion(bf16[96,81,232]{2,1,0:T(8,128)(2,1)} %bitcast.9, s32[1024]{0:T(1024)S(1)} %pad_clamp_fusion.1), kind=kCustom, calls=%fused_computation.1 | custom fusion | bytes 2706192 | tf_op jit(solution)/shard_map/jit(_take)/gather | solution.py:340
  118.0 0.2 broadcast_select_fusion.1
  118.2 1.4 pad.20.x_ref
  119.6 75.5 %film_block.1 = (bf16[36,81,384]{2,1,0:T(8,128)(2,1)}, bf16[10240,128]{1,0:T(8,128)(2,1)}) custom-call(bf16[36,81,256]{2,1,0:T(8,128)(2,1)} %pad.20.x_ref, bf16[36,512]{1,0:T(8,128)(2,1)} %broadcast_select_fusion.3.e_ref, bf16[36,81,384]{2,1,0:T(8,128)(2,1)} %bitcast.52, bf16[256,1408]{1,0:T(8,128)(2,1)} %pad.21.we_ref, ...), custom_call_target="tpu_custom_call" | custom-call | tf_op jit(solution)/shard_map/film_block/pallas_call | solution.py:149
  195.2 44.4 %grad_sum.1 = (f32[232,1392]{1,0:T(8,128)S(1)}, f32[9,1392]{1,0:T(8,128)S(1)}, f32[1392,384]{1,0:T(8,128)S(1)}, f32[512,768]{1,0:T(8,128)S(1)}) custom-call(bf16[10240,128]{1,0:T(8,128)(2,1)} %get-tuple-element.12.g_ref), custom_call_target="tpu_custom_call" | custom-call | tf_op jit(solution)/shard_map/grad_sum/pallas_call | solution.py:278
  239.6 1.1 copy.56
  240.6 0.6 copy.57
  241.3 1.3 copy.58
  242.6 1.1 copy.59
  (30 shorter events, 0.9 us)
Async XLA Ops:
  0.6 32.8 %copy-start = (bf16[8,512]{1,0:T(8,128)(2,1)S(1)}, bf16[8,512]{1,0:T(8,128)(2,1)}, u32[]{:S(2)}) copy-start(bf16[8,512]{1,0:T(8,128)(2,1)} %param.11) | copy-start | bytes 24580
  3.6 28.2 %all-to-all-start = ((s32[32,1,3]{2,1,0:T(1,128)}), s32[32,1,3]{2,1,0:T(1,128)S(1)}, u32[]{:S(2)}, u32[]{:S(2)}) async-start(s32[32,1,3]{2,1,0:T(1,128)} %bitcast.4), calls=%async_computation | async-start | bytes 32768 | tf_op jit(solution)/shard_map/all_to_all | solution.py:318
  35.1 18.6 %all-to-all-start.2 = ((bf16[32,3,512]{2,1,0:T(4,128)(2,1)}), bf16[32,3,512]{2,1,0:T(4,128)(2,1)S(1)}, u32[]{:S(2)}, u32[]{:S(2)}) async-start(bf16[32,3,512]{2,1,0:T(4,128)(2,1)} %broadcast_select_fusion.2), calls=%async_computation.2 | async-start | bytes 262144 | tf_op jit(solution)/shard_map/all_to_all | solution.py:332
  53.7 7.6 %copy-start.2 = (bf16[1392,384]{1,0:T(8,128)(2,1)S(1)}, bf16[1392,384]{1,0:T(8,128)(2,1)}, u32[]{:S(2)}) copy-start(bf16[1392,384]{1,0:T(8,128)(2,1)} %param.17) | copy-start | bytes 3207172
  53.7 61.4 %all-to-all-start.1 = ((bf16[32,3,81,232]{3,2,1,0:T(8,128)(2,1)}), bf16[32,3,81,232]{3,2,1,0:T(8,128)(2,1)}, u32[]{:S(2)}, u32[]{:S(2)}) async-start(bf16[32,3,81,232]{3,2,1,0:T(8,128)(2,1)} %broadcast_select_fusion), calls=%async_computation.1 | async-start | bytes 8650752 | tf_op jit(solution)/shard_map/all_to_all | solution.py:325
  61.3 2.4 copy-start.3
  64.9 1.1 copy-start.4
  64.9 1.1 copy-start.5
  241.3 2.5 %copy-start.1 = (bf16[8,512]{1,0:T(8,128)(2,1)S(1)}, bf16[8,512]{1,0:T(8,128)(2,1)}, u32[]{:S(2)}) copy-start(bf16[8,512]{1,0:T(8,128)(2,1)} %param.11) | copy-start | bytes 24580

commit v3 on v2

--- a/solution.py
+++ b/solution.py
@@ -1,3 +1,4 @@
+import functools
 import jax, jax.numpy as jnp
 from jax import lax
 from jax.experimental import pallas as pl
@@ -8,10 +9,121 @@
 CIN, HID, COUT, EMB, FR = 232, 1392, 384, 512, 36
 HP = 1408
 NT = 5
+ROWS = CELLS * TILE
+PEERS, RANKS, SLOT = 32, 3, 176
+EP_DEV, EP_LEN = 8, 24
 GR = 10240
 GE, GK, GP, GF = 0, 2640, 2816, 6992
-ROWS = CELLS * TILE
 f32, bf16 = jnp.float32, jnp.bfloat16
+
+
+def fetch_kernel(ask_ref, rep_ref, ins_ref, got_ref, later_ref,
+                 rep, asks, stage, out, got, rep_sem, ask_send, ask_recv, send, recv):
+    me, rail = lax.axis_index("dp"), lax.axis_index("replica")
+    load = pltpu.make_async_copy(rep_ref, rep, rep_sem)
+    load.start()
+    barrier = pltpu.get_barrier_semaphore()
+
+    def peer(d):
+        return lax.rem(me + d, PEERS)
+
+    def greet(d, c):
+        pl.semaphore_signal(barrier, inc=1, device_id=(peer(d), rail), device_id_type=pl.DeviceIdType.MESH)
+        return c
+    lax.fori_loop(1, PEERS, greet, 0)
+    pl.semaphore_wait(barrier, PEERS - 1)
+
+    def ask(d):
+        return pltpu.make_async_remote_copy(src_ref=ask_ref, dst_ref=asks.at[me], send_sem=ask_send.at[d], recv_sem=ask_recv.at[d],
+                                            device_id=(peer(d), rail), device_id_type=pl.DeviceIdType.MESH)
+
+    def frame(d):
+        return pltpu.make_async_remote_copy(src_ref=out.at[peer(d)], dst_ref=got.at[me], send_sem=send.at[d], recv_sem=recv.at[d],
+                                            device_id=(peer(d), rail), device_id_type=pl.DeviceIdType.MESH)
+
+    def each(f):
+        def body(d, c):
+            f(d)
+            return c
+        lax.fori_loop(1, PEERS, body, 0)
+    each(lambda d: ask(d).start())
+    asks[me] = ask_ref[...]
+    zero = jnp.zeros((PEERS * RANKS, 128), f32)
+    for r in range(2 * CELLS + 4, SLOT):
+        stage[pl.ds(r, PEERS * RANKS, stride=SLOT), :] = zero
+    each(lambda d: ask(d).wait_recv())
+    owner, wanted = asks[:, 0, :], asks[:, 1, :]
+    mine = owner == me
+    before = lax.broadcasted_iota(jnp.int32, (128, 128), 0) < lax.broadcasted_iota(jnp.int32, (128, 128), 1)
+    rank = jnp.dot(jnp.where(mine, 1.0, 0.0).astype(bf16), jnp.where(before, 1.0, 0.0).astype(bf16), preferred_element_type=f32)
+    wide = wanted.astype(f32)
+    picks = []
+    for k in range(RANKS):
+        hit = mine & (rank > k - 0.5) & (rank < k + 0.5)
+        picks.append(jnp.sum(jnp.where(hit, wide + 1.0, 0.0), axis=1, keepdims=True) - 1.0)
+    pick = jnp.concatenate(picks, axis=0)
+    at = lax.broadcasted_iota(jnp.int32, (PEERS * RANKS, EP_DEV * EP_LEN), 1).astype(f32)
+    choose = jnp.where(pick == at, 1.0, 0.0).astype(bf16)
+    low = lax.broadcasted_iota(jnp.int32, (PEERS * RANKS, EP_DEV), 1).astype(f32) * EP_LEN
+    which = jnp.where((pick >= low) & (pick < low + EP_LEN), 1.0, 0.0).astype(bf16)
+    words = jnp.dot(which, ins_ref[...], preferred_element_type=f32)
+
+    def put(row, values):
+        stage[pl.ds(row, PEERS, stride=SLOT), :] = values[:PEERS]
+
+    def put_later(row, values):
+        for k in range(2):
+            stage[pl.ds((PEERS + k) * SLOT + row, PEERS, stride=2 * SLOT), :] = values[k * PEERS:k * PEERS + PEERS]
+    for q in range(4):
+        put(2 * CELLS + q, words[:PEERS, q * 128:q * 128 + 128])
+        put_later(2 * CELLS + q, words[PEERS:, q * 128:q * 128 + 128])
+    load.wait()
+
+    def cells(chosen, store):
+        blank = jnp.zeros((chosen.shape[0], 256 - CIN), f32)
+
+        def some(i, carry):
+            for u in range(3):
+                c = i * 3 + u
+                found = jnp.dot(chosen, rep[:, c].reshape(EP_DEV * EP_LEN, CIN), preferred_element_type=f32)
+                store(c, found[:, :128])
+                store(CELLS + c, jnp.concatenate([found[:, 128:], blank], axis=1))
+            return carry
+        lax.fori_loop(0, CELLS // 3, some, 0)
+    cells(choose[:PEERS], put)
+
+    def pack(p, carry):
+        out[p] = stage[pl.ds(pl.multiple_of(p * SLOT, 8), SLOT), :].astype(bf16)
+        return carry
+    lax.fori_loop(0, PEERS, pack, 0)
+    each(lambda d: frame(d).start())
+    got[me] = out[me]
+    cells(choose[PEERS:], put_later)
+
+    def pack_later(p, carry):
+        later_ref[p] = stage[pl.ds(pl.multiple_of((PEERS + p) * SLOT, 8), SLOT), :].astype(bf16)
+        return carry
+    lax.fori_loop(0, 2 * PEERS, pack_later, 0)
+    each(lambda d: ask(d).wait_send())
+    each(lambda d: frame(d).wait_recv())
+    got_ref[...] = got[...]
+    each(lambda d: frame(d).wait_send())
+
+
+def fetch(asks, replay, instructions):
+    V = pl.BlockSpec(memory_space=pltpu.VMEM)
+    return pl.pallas_call(
+        fetch_kernel,
+        out_shape=(jax.ShapeDtypeStruct((PEERS, SLOT, 128), bf16), jax.ShapeDtypeStruct((2 * PEERS, SLOT, 128), bf16)),
+        in_specs=[V, pl.BlockSpec(memory_space=pl.ANY), V], out_specs=(V, V),
+        scratch_shapes=[pltpu.VMEM((EP_DEV, CELLS, EP_LEN, CIN), bf16), pltpu.VMEM((PEERS, 8, 128), jnp.int32),
+                        pltpu.VMEM((PEERS * RANKS * SLOT, 128), f32), pltpu.VMEM((PEERS, SLOT, 128), bf16),
+                        pltpu.VMEM((PEERS, SLOT, 128), bf16), pltpu.SemaphoreType.DMA,
+                        pltpu.SemaphoreType.DMA((PEERS,)), pltpu.SemaphoreType.DMA((PEERS,)),
+                        pltpu.SemaphoreType.DMA((PEERS,)), pltpu.SemaphoreType.DMA((PEERS,))],
+        compiler_params=pltpu.CompilerParams(vmem_limit_bytes=56 * 2**20, collective_id=2, has_side_effects=True),
+        name="fetch_frames",
+    )(asks, replay.transpose(0, 2, 1, 3), instructions)
 
 
 def vpu_block(lane, tile_pre, tile_sc, dw_ref, F, S1, M, sec, prec, gk_ref):
@@ -74,26 +186,68 @@
             prec[row(i * 9 + k), ln] = total * S1[row(i * 9 + k), :]
 
 
-def kernel(x_ref, e_ref, g_ref, we_ref, dw_ref, wp_ref, wpt_ref, fw_ref,
-           tok_ref, sum_ref,
-           x32, xb, g32, pc, film, pre, sc, sec, prec, secb, precb, proj, F, S1, M, fc, gpt, ge_ref, gk_ref):
-    film[FR:, :] = jnp.zeros((NT * TILE - FR, 2 * COUT), f32)
-    film[:FR, :] = jnp.dot(e_ref[...], fw_ref[...], preferred_element_type=f32)
-    gk_ref[...] = jnp.zeros_like(gk_ref)
-    ge_ref[...] = jnp.zeros_like(ge_ref)
-    gpt[...] = jnp.zeros_like(gpt)
+def sort_frames(own_ref, named, rank, order):
+    def clear(p, c):
+        named[p] = 0
+        return c
+    lax.fori_loop(0, PEERS, clear, 0)
+
+    def note(j, counts):
+        o = own_ref[j]
+        r = named[o]
+        named[o] = r + 1
+        rank[j] = r
+        return (counts[0] + (r == 0).astype(jnp.int32), counts[1] + (r == 1).astype(jnp.int32))
+    n0, n1 = lax.fori_loop(0, FR, note, (jnp.int32(0), jnp.int32(0)))
+
+    def place_frame(j, at):
+        r = rank[j]
+        p = jnp.where(r == 0, at[0], jnp.where(r == 1, at[1], at[2]))
+        order[p] = j
+        return tuple(a + (r == k).astype(jnp.int32) for k, a in enumerate(at))
+    lax.fori_loop(0, FR, place_frame, (jnp.int32(0), n0, n0 + n1))
+    return n0
+
+
+def block_kernel(last, *refs):
+    if last:
+        (own_ref, got_ref, more_ref, g_ref, we_ref, dw_ref, wp_ref, wpt_ref, fw_ref, ge0, gpt0, gk0, fc0, e0, tok0,
+         tok_ref, sum_ref, *scratch) = refs
+        (named, rank, order, x32, xb, g32, pc, e32, pre, sc, sec, prec, secb, precb, proj, F, S1, M,
+         ge, gpt, gk, fc, em) = scratch
+        fc[...] = fc0[...]
+        em[...] = e0[...]
+        tok_ref[...] = tok0[...]
+    else:
+        (own_ref, got_ref, g_ref, we_ref, dw_ref, wp_ref, wpt_ref, fw_ref,
+         ge, gpt, gk, fc, em, tok_ref, *scratch) = refs
+        (named, rank, order, x32, xb, g32, pc, e32, pre, sc, sec, prec, secb, precb, proj, F, S1, M) = scratch
+    for ref in (gk, ge, gpt):
+        ref[...] = jnp.zeros_like(ref)
+    early = sort_frames(own_ref, named, rank, order) // TILE
+    first, stop = (early, NT) if last else (0, early)
 
     def tile(ft, carry):
         for f in range(TILE):
-            j = ft * TILE + f
-            held, keep = jnp.minimum(j, FR - 1), jnp.where(j < FR, 1.0, 0.0)
+            p = ft * TILE + f
+            keep = jnp.where(p < FR, 1.0, 0.0)
+            j = order[jnp.minimum(p, FR - 1)]
+            held = got_ref[own_ref[j]]
+            if last:
+                later = more_ref[own_ref[j] * 2 + jnp.maximum(rank[j], 1) - 1]
+                held = jnp.where(rank[j] == 0, held, later)
+            held = held.astype(f32) * keep
             for l in range(2):
-                x32[l, pl.ds(f, CELLS, stride=TILE), :] = x_ref[held, :, l * 128:l * 128 + 128].astype(f32) * keep
+                x32[l, pl.ds(f, CELLS, stride=TILE), :] = held[l * CELLS:l * CELLS + CELLS]
+            for q in range(4):
+                e32[f:f + 1, q * 128:q * 128 + 128] = held[2 * CELLS + q:2 * CELLS + q + 1]
             for l in range(3):
-                g32[l, pl.ds(f, CELLS, stride=TILE), :] = g_ref[held, :, l * 128:l * 128 + 128].astype(f32) * keep
+                g32[l, pl.ds(f, CELLS, stride=TILE), :] = g_ref[j, :, l * 128:l * 128 + 128].astype(f32) * keep
         for l in range(2):
             xb[:, l * 128:l * 128 + 128] = x32[l].astype(bf16)
-        fm = film[pl.ds(pl.multiple_of(ft * TILE, TILE), TILE), :]
+        eb = e32[...].astype(bf16)
+        em[ft] = eb
+        fm = jnp.dot(eb, fw_ref[...], preferred_element_type=f32)
         scale, shift = 1.0 + fm[:, :COUT], fm[:, COUT:]
         for l in range(3):
             sl = slice(l * 128, l * 128 + 128)
@@ -102,60 +256,70 @@
         sc[...] = jnp.dot(pc[...], wpt_ref[...], preferred_element_type=f32)
 
         def lanes(lt, carry):
-            vpu_block(pl.multiple_of(lt * 128, 128), pre, sc, dw_ref, F, S1, M, sec, prec, gk_ref)
+            vpu_block(pl.multiple_of(lt * 128, 128), pre, sc, dw_ref, F, S1, M, sec, prec, gk)
             return carry
         lax.fori_loop(0, HP // 128, lanes, 0)
         secb[...] = sec[...].astype(bf16)
         precb[...] = prec[...].astype(bf16)
         pj = jnp.dot(secb[...], wp_ref[...], preferred_element_type=f32)
-        fr = pl.ds(pl.multiple_of(ft * TILE, TILE), TILE)
         for l in range(3):
             sl = slice(l * 128, l * 128 + 128)
             g3, pj3 = g32[l].reshape(CELLS, TILE, 128), pj[:, sl].reshape(CELLS, TILE, 128)
-            fc[fr, sl] = jnp.sum(g3 * pj3, axis=0)
-            fc[fr, COUT + l * 128:COUT + l * 128 + 128] = jnp.sum(g3, axis=0)
+            fc[ft, :, sl] = jnp.sum(g3 * pj3, axis=0)
+            fc[ft, :, COUT + l * 128:COUT + l * 128 + 128] = jnp.sum(g3, axis=0)
             proj[l] = (pj3 * scale[None, :, sl] + shift[None, :, sl]).reshape(ROWS, 128)
         for f in range(TILE):
             @pl.when(ft * TILE + f < FR)
             def _(f=f):
+                j = order[jnp.minimum(ft * TILE + f, FR - 1)]
                 for l in range(3):
-                    tok_ref[ft * TILE + f, :, l * 128:l * 128 + 128] = proj[l, pl.ds(f, CELLS, stride=TILE), :].astype(bf16)
+                    tok_ref[j, :, l * 128:l * 128 + 128] = proj[l, pl.ds(f, CELLS, stride=TILE), :].astype(bf16)
         tn = (((0,), (0,)), ((), ()))
-        ge_ref[...] += lax.dot_general(xb[...], precb[...], tn, preferred_element_type=f32)
+        ge[...] += lax.dot_general(xb[...], precb[...], tn, preferred_element_type=f32)
         gpt[...] += lax.dot_general(pc[...], secb[...], tn, preferred_element_type=f32)
         return carry
-    lax.fori_loop(0, NT, tile, 0)
-    gk = jnp.concatenate([jnp.sum(gk_ref[...].reshape(9, 8, HP), axis=1), jnp.zeros((7, HP), f32)], axis=0).astype(bf16)
+    lax.fori_loop(first, stop, tile, 0)
+    if not last:
+        return
+    kernel_sum = jnp.sum((gk[...] + gk0[...]).reshape(9, 8, HP), axis=1)
+    kernel_sum = jnp.concatenate([kernel_sum, jnp.zeros((7, HP), f32)], axis=0).astype(bf16)
     for lt in range(HP // 128):
         ln = slice(lt * 128, lt * 128 + 128)
-        sum_ref[GE + lt * 240:GE + lt * 240 + 240, :] = ge_ref[:240, ln].astype(bf16)
-        sum_ref[GK + lt * 16:GK + lt * 16 + 16, :] = gk[:, ln]
+        sum_ref[GE + lt * 240:GE + lt * 240 + 240, :] = (ge[:240, ln] + ge0[:240, ln]).astype(bf16)
+        sum_ref[GK + lt * 16:GK + lt * 16 + 16, :] = kernel_sum[:, ln]
     for l in range(3):
-        sum_ref[GP + l * HID:GP + l * HID + HID, :] = gpt[l * 128:l * 128 + 128, :].T[:HID].astype(bf16)
-    gf = lax.dot_general(e_ref[...], fc[:FR, :].astype(bf16), (((0,), (0,)), ((), ())), preferred_element_type=f32).astype(bf16)
+        rows = slice(l * 128, l * 128 + 128)
+        sum_ref[GP + l * HID:GP + l * HID + HID, :] = (gpt[rows, :] + gpt0[rows, :]).T[:HID].astype(bf16)
+    words = em[...].astype(f32).reshape(NT * TILE, EMB).astype(bf16)
+    cots = fc[...].reshape(NT * TILE, 2 * COUT).astype(bf16)
+    gf = lax.dot_general(words, cots, (((0,), (0,)), ((), ())), preferred_element_type=f32).astype(bf16)
     for l in range(6):
         sum_ref[GF + l * EMB:GF + l * EMB + EMB, :] = gf[:, l * 128:l * 128 + 128]
     sum_ref[GF + 6 * EMB:, :] = jnp.zeros((GR - GF - 6 * EMB, 128), bf16)
 
 
-def compute(frames, emb, g, w_expand, dw_kernel, w_project, film_weight):
-    x = jnp.pad(frames, ((0, 0), (0, 0), (0, 24)))
-    we = jnp.pad(w_expand * jnp.asarray(0.5, bf16), ((0, 24), (0, 16)))
-    wp = jnp.pad(w_project, ((0, 16), (0, 0)))
-    wpt = jnp.pad((w_project * jnp.asarray(0.5, bf16)).T, ((0, 0), (0, 16)))
-    dw = jnp.repeat(jnp.pad(dw_kernel * 0.5, ((0, 0), (0, 16))), 8, axis=0)
+def block(last, owner, arrays, state):
     V = pl.BlockSpec(memory_space=pltpu.VMEM)
-    S = lambda r, c, t=f32: pltpu.VMEM((r, c), t)
+    S = lambda *shape, t=f32: pltpu.VMEM(shape, t)
+    I = lambda n: pltpu.SMEM((n,), jnp.int32)
+    O = jax.ShapeDtypeStruct
+    held = [((256, HP), f32), ((COUT, HP), f32), ((72, HP), f32), ((NT, TILE, 2 * COUT), f32), ((NT, TILE, EMB), bf16)]
+    tok = O((FR, CELLS, COUT), bf16)
+    out_shape = (tok, O((GR, 128), bf16)) if last else tuple(O(*h) for h in held) + (tok,)
+    scratch = [I(PEERS), I(FR), I(FR), S(2, ROWS, 128), S(ROWS, 256, t=bf16), S(3, ROWS, 128), S(ROWS, COUT, t=bf16), S(TILE, EMB),
+               S(ROWS, HP), S(ROWS, HP), S(ROWS, HP), S(ROWS, HP), S(ROWS, HP, t=bf16), S(ROWS, HP, t=bf16), S(3, ROWS, 128),
+               S(ROWS, 128), S(ROWS, 128), S(ROWS, 128)]
+    if last:
+        scratch += [S(*shape, t=kind) for shape, kind in held]
     return pl.pallas_call(
-        kernel,
-        out_shape=(jax.ShapeDtypeStruct((FR, CELLS, COUT), bf16), jax.ShapeDtypeStruct((GR, 128), bf16)),
-        in_specs=[V] * 8, out_specs=(V,) * 2,
-        scratch_shapes=[pltpu.VMEM((2, ROWS, 128), f32), S(ROWS, 256, bf16), pltpu.VMEM((3, ROWS, 128), f32), S(ROWS, COUT, bf16), S(NT * TILE, 2 * COUT),
-                        S(ROWS, HP), S(ROWS, HP), S(ROWS, HP), S(ROWS, HP), S(ROWS, HP, bf16), S(ROWS, HP, bf16), pltpu.VMEM((3, ROWS, 128), f32),
-                        S(ROWS, 128), S(ROWS, 128), S(ROWS, 128), S(NT * TILE, 2 * COUT), S(COUT, HP), S(256, HP), S(72, HP)],
+        functools.partial(block_kernel, last),
+        out_shape=out_shape,
+        in_specs=[pl.BlockSpec(memory_space=pltpu.SMEM)] + [V] * (len(arrays) + len(state)), out_specs=(V,) * len(out_shape),
+        scratch_shapes=scratch,
         compiler_params=pltpu.CompilerParams(vmem_limit_bytes=60 * 2**20),
-        name="film_block",
-    )(x, emb, g, we, dw, wp, wpt, film_weight)
+        cost_estimate=pl.CostEstimate(flops=2 * 10**10, bytes_accessed=2 * 10**8, transcendentals=8 * 10**6),
+        name="late_frames" if last else "early_frames",
+    )(owner, *arrays, *state)
 
 
 PIECES = (32, 32, 16)
@@ -288,80 +452,24 @@
     )(g)
 
 
-def per_device(
-    replay,
-    instructions,
-    owners,
-    episode_rows,
-    frame_steps,
-    w_expand,
-    dw_kernel,
-    w_project,
-    film_weight,
-    token_grad,
-):
-    peer_count = lax.axis_size("dp")
-    frame_count = owners.shape[0]
-    capacity = max(2, (2 * frame_count + peer_count - 1) // peer_count)
-    slot_count = peer_count * capacity
-    episode_length = replay.shape[1]
-    cell_count = replay.shape[2]
-    out_width = w_project.shape[1]
-    owner_ids = owners[:, 0]
-    positions = jnp.arange(frame_count, dtype=jnp.int32)
-    earlier = (owner_ids[:, None] == owner_ids[None, :]) & (positions[:, None] < positions[None, :])
-    rank_within = jnp.sum(earlier.astype(jnp.int32), axis=0)
-    target = owner_ids * capacity + rank_within
-    onehot = target[:, None] == jnp.arange(slot_count, dtype=jnp.int32)[None, :]
-    wanted = episode_rows * episode_length + frame_steps
-    request = jnp.sum(jnp.where(onehot, wanted[:, None], 0), axis=0).reshape(peer_count, capacity)
-    asked_rows = lax.all_to_all(request, "dp", split_axis=0, concat_axis=0, tiled=True).reshape(
-        slot_count
-    )
-    stored = replay.reshape(-1, cell_count, replay.shape[3])
-    picked = jnp.take(stored, asked_rows, axis=0)
-    picked_embedding = jnp.take(instructions, asked_rows // episode_length, axis=0)
-    arrived, arrived_embedding = (
-        lax.all_to_all(
-            picked.reshape(peer_count, capacity, cell_count, -1),
-            "dp",
-            split_axis=0,
-            concat_axis=0,
-            tiled=True,
-        ),
-        lax.all_to_all(
-            picked_embedding.reshape(peer_count, capacity, -1),
-            "dp",
-            split_axis=0,
-            concat_axis=0,
-            tiled=True,
-        ),
-    )
-    frames = jnp.take(arrived.reshape(slot_count, cell_count, -1), target, axis=0)
-    embedding = jnp.take(arrived_embedding.reshape(slot_count, -1), target, axis=0)
-    cotangent = token_grad.reshape(frame_count, cell_count, out_width)
-    tokens, partial_sums = compute(
-        frames, embedding, cotangent, w_expand, dw_kernel, w_project, film_weight
-    )
-    tokens_out = tokens.reshape(token_grad.shape)
-    summed = all_reduce(partial_sums)
-    return (tokens_out, summed[0], summed[1], summed[2], summed[3])
+def per_device(replay, instructions, owners, episode_rows, frame_steps, w_expand, dw_kernel, w_project, film_weight, token_grad):
+    owner = owners[:, 0]
+    asks = jnp.stack([jnp.pad(owner, (0, 128 - FR), constant_values=-1), jnp.pad(episode_rows * EP_LEN + frame_steps, (0, 128 - FR))])
+    asks = jnp.pad(asks, ((0, 6), (0, 0)))
+    got, later = fetch(asks, replay, instructions)
+    more = lax.all_to_all(later.reshape(PEERS, 2, SLOT, 128), "dp", split_axis=0, concat_axis=0, tiled=True).reshape(2 * PEERS, SLOT, 128)
+    g = token_grad.reshape(FR, CELLS, COUT)
+    we = jnp.pad(w_expand * jnp.asarray(0.5, bf16), ((0, 256 - CIN), (0, HP - HID)))
+    wp = jnp.pad(w_project, ((0, HP - HID), (0, 0)))
+    wpt = jnp.pad((w_project * jnp.asarray(0.5, bf16)).T, ((0, 0), (0, HP - HID)))
+    dw = jnp.repeat(jnp.pad(dw_kernel * 0.5, ((0, 0), (0, HP - HID))), 8, axis=0)
+    weights = (g, we, dw, wp, wpt, film_weight)
+    state = block(False, owner, (got,) + weights, ())
+    tokens, partial_sums = block(True, owner, (got, more) + weights, state)
+    return (tokens.reshape(token_grad.shape), *all_reduce(partial_sums))
 
 
 def solution(mesh):
-    in_specs = (
-        P(("dp", "replica"), None, None, None),
-        P(("dp", "replica"), None),
-        P(("dp", "replica"), None),
-        P(("dp", "replica")),
-        P(("dp", "replica")),
-        P(),
-        P(),
-        P(),
-        P(),
-        P(("dp", "replica"), None, None, None),
-    )
-    out_specs = (P(("dp", "replica"), None, None, None), P(), P(), P(), P())
-    return jax.shard_map(
-        per_device, mesh=mesh, in_specs=in_specs, out_specs=out_specs, check_vma=False
-    )
+    split = ("dp", "replica")
+    in_specs = (P(split), P(split), P(split), P(split), P(split), P(), P(), P(), P(), P(split))
+    return jax.shard_map(per_device, mesh=mesh, in_specs=in_specs, out_specs=(P(split), P(), P(), P(), P()), check_vma=False)

time: 244 us -> 199 us (0.82)
  Pallas kernels: 120 us -> 176 us
  waiting for transfers between devices: 46.9 us -> 0.01 us
  local copies, waits for them, and re-layouts: 42 us -> 11.7 us
  starting transfers between devices: 24.6 us -> 9.14 us
  other arithmetic: 9.56 us -> 0.87 us
    pallas_call x1 -> x3, Pallas kernels: 75.5 us -> 132 us  [the longest x2 88.3 us: block(): pl.pallas_call(functools.partial(block_kernel, last), out_shape=out_shape...]
    all_to_all x3 -> x1, waiting for transfers between devices: 46.9 us -> 0.01 us  [per_device(): lax.all_to_all(later.reshape(PEERS, 2, SLOT, 128), 'dp', split_axis=0, co...]
    all_to_all x3 -> x1, starting transfers between devices: 24.6 us -> 9.14 us  [per_device(): lax.all_to_all(later.reshape(PEERS, 2, SLOT, 128), 'dp', split_axis=0, co...]
    reshape x4 -> x1, local copies, waits for them, and re-layouts: 12.1 us -> 0.79 us  [per_device(): jnp.repeat(jnp.pad(dw_kernel * 0.5, ((0, 0), (0, HP - HID))), 8, axis=0)]
    gather x5 -> x0, local copies, waits for them, and re-layouts: 10.9 us -> none  [the longest x1 6.51 us: per_device(): picked = jnp.take(stored, asked_rows, axis=0)]
    select_n x6 -> x0, other arithmetic: 7.05 us -> none  [the longest x1 4.68 us: per_device(): picked = jnp.take(stored, asked_rows, axis=0)]
    unnamed x18 -> x11, local copies, waits for them, and re-layouts: 12.9 us -> 6.57 us
  transfers between devices with their start and end apart: 3 -> 1, of which waited for: 1 -> 0; matrix products, arithmetic and copies ran while one was open for 15% -> 3% of each run, Pallas kernels for 0% -> 32%
where the time goes in v3:
time: 199 us
  Pallas kernels  176 us (88%)
  local copies, waits for them, and re-layouts  11.7 us (6%)
  starting transfers between devices  9.14 us (5%)
    pallas_call x2, Pallas kernels, block(): pl.pallas_call(functools.partial(block_kernel, last), out_shape=out_shape...  88.3 us
    pallas_call x1, Pallas kernels, fetch(): pl.pallas_call(fetch_kernel, out_shape=(jax.ShapeDtypeStruct((PEERS, SLOT...  44.2 us
    pallas_call x1, Pallas kernels, all_reduce(): pl.pallas_call(reduce_kernel, out_shape=(jax.ShapeDtypeStruct((CIN, HID),...  43.9 us
    all_to_all x1, starting transfers between devices, per_device(): lax.all_to_all(later.reshape(PEERS, 2, SLOT, 128), 'dp', split_axis=0, co...  9.14 us
    unnamed x11, local copies, waits for them, and re-layouts  6.57 us
  transfers between devices with their start and end apart: 1, of which 0 were waited for; matrix products, arithmetic and copies ran while one was open for 3% of the time, Pallas kernels for 32%

profile of v3, /device:TPU:1, one launch (start us, length us, event | category | flops | bytes accessed | tf_op | source)
XLA Modules:
  0.0 198.9 jit_solution(11860763021607166103)
XLA Ops:
  0.6 0.7 multiply_add_fusion
  1.3 0.7 pad_bitcast_fusion
  2.0 0.6 pad.29.ask_ref
  2.6 44.2 %fetch_frames.1 = (bf16[32,176,128]{2,1,0:T(8,128)(2,1)}, bf16[64,176,128]{2,1,0:T(8,128)(2,1)}) custom-call(s32[8,128]{1,0:T(8,128)} %pad.29.ask_ref, bf16[8,81,24,232]{3,2,1,0:T(8,128)(2,1)} %bitcast.14, bf16[8,512]{1,0:T(8,128)(2,1)} %ins_ref.1), custom_call_target="tpu_custom_call" | custom-call | tf_op jit(solution)/shard_map/fetch_frames/pallas_call | solution.py:115
  46.7 0.0 copy-start.1
  46.8 9.1 %all-to-all-start = ((bf16[32,2,176,128]{3,2,1,0:T(8,128)(2,1)}), bf16[32,2,176,128]{3,2,1,0:T(8,128)(2,1)}, u32[]{:S(2)}, u32[]{:S(2)}) async-start(bf16[32,2,176,128]{3,2,1,0:T(8,128)(2,1)} %bitcast.15), calls=%async_computation | async-start | bytes 5767168 | tf_op jit(solution)/shard_map/all_to_all | solution.py:460
  55.9 0.0 copy-done.1
  55.9 0.0 copy-start
  55.9 0.1 broadcast_multiply_fusion
  56.0 1.1 copy-done
  57.1 1.2 copy.16
  58.4 1.1 pad.32.refs_5_.refs_6_
  59.5 0.9 pad.30.refs_3_.refs_4_
  60.4 0.1 multiply_bitcast_fusion
  60.5 0.0 copy-start.2
  60.6 1.1 pad.33.refs_6_.refs_7_
  61.6 0.0 copy-done.2
  61.7 0.8 broadcast_bitcast_fusion.refs_4_.refs_5_
  62.4 64.0 %early_frames.1 = (f32[256,1408]{1,0:T(8,128)}, f32[384,1408]{1,0:T(8,128)}, f32[72,1408]{1,0:T(8,128)}, f32[5,8,768]{2,1,0:T(8,128)}, bf16[5,8,512]{2,1,0:T(8,128)(2,1)}, /*index=5*/bf16[36,81,384]{2,1,0:T(8,128)(2,1)}) custom-call(s32[36]{0:T(128)} %bitcast.17, bf16[32,176,128]{2,1,0:T(8,128)(2,1)} %get-tuple-element.19.refs_1_, ...), custom_call_target="tpu_custom_call" | custom-call | flops 20000000000 | bytes 200000000 | tf_op jit(solution)/shard_map/early_frames/pallas_call | solution.py:314
  126.4 0.0 all-to-all-done
  126.4 24.3 %late_frames.1 = (bf16[36,81,384]{2,1,0:T(8,128)(2,1)}, bf16[10240,128]{1,0:T(8,128)(2,1)}) custom-call(s32[36]{0:T(128)} %bitcast.18, bf16[32,176,128]{2,1,0:T(8,128)(2,1)} %get-tuple-element.19.refs_1_, bf16[64,176,128]{2,1,0:T(8,128)(2,1)} %bitcast.5.refs_2_, bf16[36,81,384]{2,1,0:T(8,128)(2,1)} %bitcast.20, bf16[256,1408]{1,0:T(8,128)(2,1)} %pad.30.refs_3_.refs_4_, ...), custom_call_target="tpu_custom_call" | custom-call | flops 20000000000 | bytes 200000000 | tf_op jit(solution)/shard_map/late_frames/pallas_call | solution.py:314
  150.8 43.9 %grad_sum.1 = (f32[232,1392]{1,0:T(8,128)S(1)}, f32[9,1392]{1,0:T(8,128)S(1)}, f32[1392,384]{1,0:T(8,128)S(1)}, f32[512,768]{1,0:T(8,128)S(1)}) custom-call(bf16[10240,128]{1,0:T(8,128)(2,1)} %get-tuple-element.28.g_ref), custom_call_target="tpu_custom_call" | custom-call | tf_op jit(solution)/shard_map/grad_sum/pallas_call | solution.py:442
  194.7 1.1 copy.22
  195.8 0.6 copy.23
  196.4 1.3 copy.24
  197.7 1.1 copy.25
  (3 shorter events, 0.0 us)
Async XLA Ops:
  46.7 9.2 %copy-start.1 = (bf16[232,1392]{1,0:T(8,128)(2,1)S(1)}, bf16[232,1392]{1,0:T(8,128)(2,1)}, u32[]{:S(2)}) copy-start(bf16[232,1392]{1,0:T(8,128)(2,1)} %param.15) | copy-start | bytes 1937668
  46.8 79.7 %all-to-all-start = ((bf16[32,2,176,128]{3,2,1,0:T(8,128)(2,1)}), bf16[32,2,176,128]{3,2,1,0:T(8,128)(2,1)}, u32[]{:S(2)}, u32[]{:S(2)}) async-start(bf16[32,2,176,128]{3,2,1,0:T(8,128)(2,1)} %bitcast.15), calls=%async_computation | async-start | bytes 5767168 | tf_op jit(solution)/shard_map/all_to_all | solution.py:460
  55.9 1.2 copy-start
  60.5 1.1 copy-start.2

commit v4 on v3

--- a/solution.py
+++ b/solution.py
@@ -8,6 +8,7 @@
 SIDE, CELLS, TILE = 9, 81, 8
 CIN, HID, COUT, EMB, FR = 232, 1392, 384, 512, 36
 HP = 1408
+NL = HP // 128
 NT = 5
 ROWS = CELLS * TILE
 PEERS, RANKS, SLOT = 32, 3, 176
@@ -17,11 +18,14 @@
 f32, bf16 = jnp.float32, jnp.bfloat16
 
 
-def fetch_kernel(ask_ref, rep_ref, ins_ref, got_ref, later_ref,
-                 rep, asks, stage, out, got, rep_sem, ask_send, ask_recv, send, recv):
+def fetch_kernel(own_ref, row_ref, step_ref, rep_ref, ins_ref, got_ref, later_ref,
+                 rep, ask_ref, asks, stage, out, got, rep_sem, ask_send, ask_recv, send, recv):
     me, rail = lax.axis_index("dp"), lax.axis_index("replica")
     load = pltpu.make_async_copy(rep_ref, rep, rep_sem)
     load.start()
+    ask_ref[...] = jnp.full((8, 128), -1, jnp.int32)
+    ask_ref[0:1, :FR] = own_ref[...]
+    ask_ref[1:2, :FR] = row_ref[...] * EP_LEN + step_ref[...]
     barrier = pltpu.get_barrier_semaphore()
 
     def peer(d):
@@ -110,80 +114,70 @@
     each(lambda d: frame(d).wait_send())
 
 
-def fetch(asks, replay, instructions):
+def fetch(owner, row, step, replay, instructions):
     V = pl.BlockSpec(memory_space=pltpu.VMEM)
     return pl.pallas_call(
         fetch_kernel,
         out_shape=(jax.ShapeDtypeStruct((PEERS, SLOT, 128), bf16), jax.ShapeDtypeStruct((2 * PEERS, SLOT, 128), bf16)),
-        in_specs=[V, pl.BlockSpec(memory_space=pl.ANY), V], out_specs=(V, V),
-        scratch_shapes=[pltpu.VMEM((EP_DEV, CELLS, EP_LEN, CIN), bf16), pltpu.VMEM((PEERS, 8, 128), jnp.int32),
+        in_specs=[V, V, V, pl.BlockSpec(memory_space=pl.ANY), V], out_specs=(V, V),
+        scratch_shapes=[pltpu.VMEM((EP_DEV, CELLS, EP_LEN, CIN), bf16), pltpu.VMEM((8, 128), jnp.int32), pltpu.VMEM((PEERS, 8, 128), jnp.int32),
                         pltpu.VMEM((PEERS * RANKS * SLOT, 128), f32), pltpu.VMEM((PEERS, SLOT, 128), bf16),
                         pltpu.VMEM((PEERS, SLOT, 128), bf16), pltpu.SemaphoreType.DMA,
                         pltpu.SemaphoreType.DMA((PEERS,)), pltpu.SemaphoreType.DMA((PEERS,)),
                         pltpu.SemaphoreType.DMA((PEERS,)), pltpu.SemaphoreType.DMA((PEERS,))],
         compiler_params=pltpu.CompilerParams(vmem_limit_bytes=56 * 2**20, collective_id=2, has_side_effects=True),
         name="fetch_frames",
-    )(asks, replay.transpose(0, 2, 1, 3), instructions)
-
-
-def vpu_block(lane, tile_pre, tile_sc, dw_ref, F, S1, M, sec, prec, gk_ref):
-    ln = pl.ds(lane, 128)
+    )(owner, row, step, replay.transpose(0, 2, 1, 3), instructions)
+
+
+def vpu_block(pre, sc, dw_ref, F, S1, M, sec, prec, gk_ref):
     row = lambda c: slice(c * 8, c * 8 + 8)
-    for c in range(CELLS):
-        h = tile_pre[row(c), ln]
-        t = jnp.tanh(h)
-        u = 1.0 + t
-        F[row(c), :] = h * u
-        S1[row(c), :] = u * (1.0 + h * (1.0 - t))
-    taps = [dw_ref[t * 8:t * 8 + 8, ln] for t in range(9)]
-    acc = [gk_ref[t * 8:t * 8 + 8, ln] for t in range(9)]
-    get = lambda ref, i: [ref[row(i * 9 + k), :] for k in range(9)]
-    prev, cur, nxt = None, None, get(F, 0)
-    for i in range(9):
-        prev, cur = cur, nxt
-        nxt = get(F, i + 1) if i < 8 else None
-        rows3 = (prev, cur, nxt)
+    tap = lambda t: dw_ref[t * 8:t * 8 + 8, :]
+    acc = [gk_ref[t * 8:t * 8 + 8, :] for t in range(9)]
+    get = lambda ref, i: [ref[row(i * 9 + k), :] for k in range(9)] if 0 <= i < 9 else None
+
+    def activate(i):
+        for k in range(9):
+            c = i * 9 + k
+            h = pre[row(c), :]
+            t = jnp.tanh(h)
+            u = 1.0 + t
+            F[row(c), :] = (h * u).astype(bf16).astype(f32)
+            S1[row(c), :] = u * (1.0 + h * (1.0 - t))
+
+    def ahead(i):
+        rows3 = (get(F, i - 1), get(F, i), get(F, i + 1))
+        for k in range(9):
+            near = [(3 * r + c, rows3[r][k + c - 1]) for r in range(3) if rows3[r] for c in range(3) if 0 <= k + c - 1 < 9]
+            h = None
+            for t, v in near:
+                h = tap(t) * v if h is None else h + tap(t) * v
+            t = jnp.tanh(h)
+            u = 1.0 + t
+            sec[row(i * 9 + k), :] = h * u
+            mc = sc[row(i * 9 + k), :] * (u * (1.0 + h * (1.0 - t)))
+            M[row(i * 9 + k), :] = mc
+            for t, v in near:
+                acc[t] = acc[t] + mc * v
+
+    def back(i):
+        rows3 = (get(M, i + 1), get(M, i), get(M, i - 1))
         for k in range(9):
             total = None
             for r in range(3):
-                if rows3[r] is None:
-                    continue
                 for c in range(3):
-                    kk = k + c - 1
-                    if 0 <= kk < 9:
-                        term = taps[3 * r + c] * rows3[r][kk]
+                    if rows3[r] and 0 <= k - c + 1 < 9:
+                        term = tap(3 * r + c) * rows3[r][k - c + 1]
                         total = term if total is None else total + term
-            h = total
-            t = jnp.tanh(h)
-            u = 1.0 + t
-            sec[row(i * 9 + k), ln] = h * u
-            mc = tile_sc[row(i * 9 + k), ln] * (u * (1.0 + h * (1.0 - t)))
-            M[row(i * 9 + k), :] = mc
-            for r in range(3):
-                if rows3[r] is None:
-                    continue
-                for c in range(3):
-                    kk = k + c - 1
-                    if 0 <= kk < 9:
-                        acc[3 * r + c] = acc[3 * r + c] + mc * rows3[r][kk]
+            prec[row(i * 9 + k), :] = total * S1[row(i * 9 + k), :]
+    for i in range(9):
+        activate(i)
+    for i in range(9):
+        ahead(i)
+    for i in range(9):
+        back(i)
     for t in range(9):
-        gk_ref[t * 8:t * 8 + 8, ln] = acc[t]
-    prev, cur, nxt = None, None, get(M, 0)
-    for i in range(9):
-        prev, cur = cur, nxt
-        nxt = get(M, i + 1) if i < 8 else None
-        rows3 = (nxt, cur, prev)
-        for k in range(9):
-            total = None
-            for r in range(3):
-                if rows3[r] is None:
-                    continue
-                for c in range(3):
-                    kk = k - c + 1
-                    if 0 <= kk < 9:
-                        term = taps[3 * r + c] * rows3[r][kk]
-                        total = term if total is None else total + term
-            prec[row(i * 9 + k), ln] = total * S1[row(i * 9 + k), :]
+        gk_ref[t * 8:t * 8 + 8, :] = acc[t]
 
 
 def sort_frames(own_ref, named, rank, order):
@@ -209,19 +203,34 @@
     return n0
 
 
+def prepare(wx_ref, kern_ref, wj_ref, we, dw, wp, wpt):
+    we[...] = jnp.zeros_like(we)
+    we[:CIN, :HID] = wx_ref[...] * jnp.asarray(0.5, bf16)
+    wp[:HID, :] = wj_ref[...]
+    wp[HID:, :] = jnp.zeros((HP - HID, COUT), bf16)
+    wpt[...] = wp[...].T * jnp.asarray(0.5, bf16)
+    taps = jnp.concatenate([kern_ref[...] * 0.5, jnp.zeros((9, HP - HID), f32)], axis=1)
+    for k in range(NL):
+        for t in range(9):
+            dw[k, t * 8:t * 8 + 8, :] = jnp.broadcast_to(taps[t:t + 1, k * 128:k * 128 + 128], (8, 128))
+
+
 def block_kernel(last, *refs):
     if last:
-        (own_ref, got_ref, more_ref, g_ref, we_ref, dw_ref, wp_ref, wpt_ref, fw_ref, ge0, gpt0, gk0, fc0, e0, tok0,
+        (own_ref, got_ref, g_ref, fw_ref, more_ref, we_ref, dw_ref, wp_ref, wpt_ref, fc0, e0, ge0, gpt0, gk0, tok0,
          tok_ref, sum_ref, *scratch) = refs
-        (named, rank, order, x32, xb, g32, pc, e32, pre, sc, sec, prec, secb, precb, proj, F, S1, M,
-         ge, gpt, gk, fc, em) = scratch
+        (named, rank, order, x32, xb, g32, pc, e32, pre, sc, sec, prec, secb, precb, proj, F, S1, M, tokens, tok_sem,
+         ge, gpt, gk, fc, em, ge1, gpt1, gk1, sums_sem) = scratch
+        loads = [pltpu.make_async_copy(src, dst, sums_sem.at[n]) for n, (src, dst) in enumerate(((ge0, ge1), (gpt0, gpt1), (gk0, gk1)))]
+        for load in loads:
+            load.start()
         fc[...] = fc0[...]
         em[...] = e0[...]
-        tok_ref[...] = tok0[...]
     else:
-        (own_ref, got_ref, g_ref, we_ref, dw_ref, wp_ref, wpt_ref, fw_ref,
-         ge, gpt, gk, fc, em, tok_ref, *scratch) = refs
-        (named, rank, order, x32, xb, g32, pc, e32, pre, sc, sec, prec, secb, precb, proj, F, S1, M) = scratch
+        (own_ref, got_ref, g_ref, fw_ref, wx_ref, kern_ref, wj_ref,
+         we_ref, dw_ref, wp_ref, wpt_ref, fc, em, ge, gpt, gk, tok_ref, *scratch) = refs
+        (named, rank, order, x32, xb, g32, pc, e32, pre, sc, sec, prec, secb, precb, proj, F, S1, M, tokens, tok_sem) = scratch
+        prepare(wx_ref, kern_ref, wj_ref, we_ref, dw_ref, wp_ref, wpt_ref)
     for ref in (gk, ge, gpt):
         ref[...] = jnp.zeros_like(ref)
     early = sort_frames(own_ref, named, rank, order) // TILE
@@ -252,15 +261,25 @@
         for l in range(3):
             sl = slice(l * 128, l * 128 + 128)
             pc[:, sl] = (g32[l].reshape(CELLS, TILE, 128) * scale[None, :, sl]).reshape(ROWS, 128).astype(bf16)
-        pre[...] = jnp.dot(xb[...], we_ref[...], preferred_element_type=f32)
-        sc[...] = jnp.dot(pc[...], wpt_ref[...], preferred_element_type=f32)
-
-        def lanes(lt, carry):
-            vpu_block(pl.multiple_of(lt * 128, 128), pre, sc, dw_ref, F, S1, M, sec, prec, gk)
+        hidden = jnp.dot(xb[...], we_ref[...], preferred_element_type=f32)
+        for k in range(NL):
+            pre[k] = hidden[:, k * 128:k * 128 + 128]
+        hidden = jnp.dot(pc[...], wpt_ref[...], preferred_element_type=f32)
+        for k in range(NL):
+            sc[k] = hidden[:, k * 128:k * 128 + 128]
+
+        def one(k, n):
+            vpu_block(pre.at[k], sc.at[k], dw_ref.at[k], F.at[n], S1.at[n], M.at[n], sec.at[k], prec.at[k], gk.at[k])
+
+        def lanes(i, carry):
+            one(2 * i, 0)
+            one(2 * i + 1, 1)
             return carry
-        lax.fori_loop(0, HP // 128, lanes, 0)
-        secb[...] = sec[...].astype(bf16)
-        precb[...] = prec[...].astype(bf16)
+        lax.fori_loop(0, NL // 2, lanes, 0)
+        one(NL - 1, 0)
+        for k in range(NL):
+            secb[:, k * 128:k * 128 + 128] = sec[k].astype(bf16)
+            precb[:, k * 128:k * 128 + 128] = prec[k].astype(bf16)
         pj = jnp.dot(secb[...], wp_ref[...], preferred_element_type=f32)
         for l in range(3):
             sl = slice(l * 128, l * 128 + 128)
@@ -268,28 +287,37 @@
             fc[ft, :, sl] = jnp.sum(g3 * pj3, axis=0)
             fc[ft, :, COUT + l * 128:COUT + l * 128 + 128] = jnp.sum(g3, axis=0)
             proj[l] = (pj3 * scale[None, :, sl] + shift[None, :, sl]).reshape(ROWS, 128)
+        def token_copy(f):
+            j = order[jnp.minimum(ft * TILE + f, FR - 1)]
+            return pltpu.make_async_copy(tokens.at[f], tok_ref.at[j], tok_sem.at[f])
+        for f in range(TILE):
+            for l in range(3):
+                tokens[f, :, l * 128:l * 128 + 128] = proj[l, pl.ds(f, CELLS, stride=TILE), :].astype(bf16)
+
+            @pl.when(ft * TILE + f < FR)
+            def _(f=f):
+                token_copy(f).start()
+        tn = (((0,), (0,)), ((), ()))
+        ge[...] += lax.dot_general(xb[...], precb[...], tn, preferred_element_type=f32)
+        gpt[...] += lax.dot_general(pc[...], secb[...], tn, preferred_element_type=f32)
         for f in range(TILE):
             @pl.when(ft * TILE + f < FR)
             def _(f=f):
-                j = order[jnp.minimum(ft * TILE + f, FR - 1)]
-                for l in range(3):
-                    tok_ref[j, :, l * 128:l * 128 + 128] = proj[l, pl.ds(f, CELLS, stride=TILE), :].astype(bf16)
-        tn = (((0,), (0,)), ((), ()))
-        ge[...] += lax.dot_general(xb[...], precb[...], tn, preferred_element_type=f32)
-        gpt[...] += lax.dot_general(pc[...], secb[...], tn, preferred_element_type=f32)
+                token_copy(f).wait()
         return carry
     lax.fori_loop(first, stop, tile, 0)
     if not last:
         return
-    kernel_sum = jnp.sum((gk[...] + gk0[...]).reshape(9, 8, HP), axis=1)
-    kernel_sum = jnp.concatenate([kernel_sum, jnp.zeros((7, HP), f32)], axis=0).astype(bf16)
-    for lt in range(HP // 128):
-        ln = slice(lt * 128, lt * 128 + 128)
-        sum_ref[GE + lt * 240:GE + lt * 240 + 240, :] = (ge[:240, ln] + ge0[:240, ln]).astype(bf16)
-        sum_ref[GK + lt * 16:GK + lt * 16 + 16, :] = kernel_sum[:, ln]
+    for load in loads:
+        load.wait()
+    for k in range(NL):
+        ln = slice(k * 128, k * 128 + 128)
+        sum_ref[GE + k * 240:GE + k * 240 + 240, :] = (ge[:240, ln] + ge1[:240, ln]).astype(bf16)
+        taps = jnp.sum((gk[k] + gk1[k]).reshape(9, 8, 128), axis=1)
+        sum_ref[GK + k * 16:GK + k * 16 + 16, :] = jnp.concatenate([taps, jnp.zeros((7, 128), f32)], axis=0).astype(bf16)
     for l in range(3):
         rows = slice(l * 128, l * 128 + 128)
-        sum_ref[GP + l * HID:GP + l * HID + HID, :] = (gpt[rows, :] + gpt0[rows, :]).T[:HID].astype(bf16)
+        sum_ref[GP + l * HID:GP + l * HID + HID, :] = (gpt[rows, :] + gpt1[rows, :]).T[:HID].astype(bf16)
     words = em[...].astype(f32).reshape(NT * TILE, EMB).astype(bf16)
     cots = fc[...].reshape(NT * TILE, 2 * COUT).astype(bf16)
     gf = lax.dot_general(words, cots, (((0,), (0,)), ((), ())), preferred_element_type=f32).astype(bf16)
@@ -298,28 +326,34 @@
     sum_ref[GF + 6 * EMB:, :] = jnp.zeros((GR - GF - 6 * EMB, 128), bf16)
 
 
-def block(last, owner, arrays, state):
-    V = pl.BlockSpec(memory_space=pltpu.VMEM)
+def block(last, owner, arrays):
+    V, A = pl.BlockSpec(memory_space=pltpu.VMEM), pl.BlockSpec(memory_space=pl.ANY)
     S = lambda *shape, t=f32: pltpu.VMEM(shape, t)
     I = lambda n: pltpu.SMEM((n,), jnp.int32)
     O = jax.ShapeDtypeStruct
-    held = [((256, HP), f32), ((COUT, HP), f32), ((72, HP), f32), ((NT, TILE, 2 * COUT), f32), ((NT, TILE, EMB), bf16)]
+    weights = [((256, HP), bf16), ((NL, 72, 128), f32), ((HP, COUT), bf16), ((COUT, HP), bf16)]
+    frames = [((NT, TILE, 2 * COUT), f32), ((NT, TILE, EMB), bf16)]
+    sums = [((256, HP), f32), ((COUT, HP), f32), ((NL, 72, 128), f32)]
     tok = O((FR, CELLS, COUT), bf16)
-    out_shape = (tok, O((GR, 128), bf16)) if last else tuple(O(*h) for h in held) + (tok,)
     scratch = [I(PEERS), I(FR), I(FR), S(2, ROWS, 128), S(ROWS, 256, t=bf16), S(3, ROWS, 128), S(ROWS, COUT, t=bf16), S(TILE, EMB),
-               S(ROWS, HP), S(ROWS, HP), S(ROWS, HP), S(ROWS, HP), S(ROWS, HP, t=bf16), S(ROWS, HP, t=bf16), S(3, ROWS, 128),
-               S(ROWS, 128), S(ROWS, 128), S(ROWS, 128)]
+               S(NL, ROWS, 128), S(NL, ROWS, 128), S(NL, ROWS, 128), S(NL, ROWS, 128), S(ROWS, HP, t=bf16), S(ROWS, HP, t=bf16),
+               S(3, ROWS, 128), S(2, ROWS, 128), S(2, ROWS, 128), S(2, ROWS, 128), S(TILE, CELLS, COUT, t=bf16), pltpu.SemaphoreType.DMA((TILE,))]
+    smem = pl.BlockSpec(memory_space=pltpu.SMEM)
     if last:
-        scratch += [S(*shape, t=kind) for shape, kind in held]
+        out_shape, out_specs = (tok, O((GR, 128), bf16)), (A, V)
+        in_specs = [smem] + [V] * 10 + [A] * 4
+        scratch += [S(*shape, t=kind) for shape, kind in sums + frames + sums] + [pltpu.SemaphoreType.DMA((3,))]
+        aliases = {14: 0}
+    else:
+        out_shape = tuple(O(*h) for h in weights + frames + sums) + (tok,)
+        out_specs, in_specs, aliases = (V,) * 9 + (A,), [smem] + [V] * 6, {}
     return pl.pallas_call(
         functools.partial(block_kernel, last),
-        out_shape=out_shape,
-        in_specs=[pl.BlockSpec(memory_space=pltpu.SMEM)] + [V] * (len(arrays) + len(state)), out_specs=(V,) * len(out_shape),
-        scratch_shapes=scratch,
-        compiler_params=pltpu.CompilerParams(vmem_limit_bytes=60 * 2**20),
+        out_shape=out_shape, in_specs=in_specs, out_specs=out_specs, scratch_shapes=scratch, input_output_aliases=aliases,
+        compiler_params=pltpu.CompilerParams(vmem_limit_bytes=61 * 2**20),
         cost_estimate=pl.CostEstimate(flops=2 * 10**10, bytes_accessed=2 * 10**8, transcendentals=8 * 10**6),
         name="late_frames" if last else "early_frames",
-    )(owner, *arrays, *state)
+    )(owner, *arrays)
 
 
 PIECES = (32, 32, 16)
@@ -454,18 +488,11 @@
 
 def per_device(replay, instructions, owners, episode_rows, frame_steps, w_expand, dw_kernel, w_project, film_weight, token_grad):
     owner = owners[:, 0]
-    asks = jnp.stack([jnp.pad(owner, (0, 128 - FR), constant_values=-1), jnp.pad(episode_rows * EP_LEN + frame_steps, (0, 128 - FR))])
-    asks = jnp.pad(asks, ((0, 6), (0, 0)))
-    got, later = fetch(asks, replay, instructions)
+    got, later = fetch(owner.reshape(1, FR), episode_rows.reshape(1, FR), frame_steps.reshape(1, FR), replay, instructions)
     more = lax.all_to_all(later.reshape(PEERS, 2, SLOT, 128), "dp", split_axis=0, concat_axis=0, tiled=True).reshape(2 * PEERS, SLOT, 128)
     g = token_grad.reshape(FR, CELLS, COUT)
-    we = jnp.pad(w_expand * jnp.asarray(0.5, bf16), ((0, 256 - CIN), (0, HP - HID)))
-    wp = jnp.pad(w_project, ((0, HP - HID), (0, 0)))
-    wpt = jnp.pad((w_project * jnp.asarray(0.5, bf16)).T, ((0, 0), (0, HP - HID)))
-    dw = jnp.repeat(jnp.pad(dw_kernel * 0.5, ((0, 0), (0, HP - HID))), 8, axis=0)
-    weights = (g, we, dw, wp, wpt, film_weight)
-    state = block(False, owner, (got,) + weights, ())
-    tokens, partial_sums = block(True, owner, (got, more) + weights, state)
+    *weights, cots, words, grad_e, grad_p, grad_k, tokens = block(False, owner, (got, g, film_weight, w_expand, dw_kernel, w_project))
+    tokens, partial_sums = block(True, owner, (got, g, film_weight, more, *weights, cots, words, grad_e, grad_p, grad_k, tokens))
     return (tokens.reshape(token_grad.shape), *all_reduce(partial_sums))
 
 

time: 199 us -> 183 us (0.920)
  Pallas kernels: 176 us -> 167 us
  local copies, waits for them, and re-layouts: 11.7 us -> 5.74 us
    pallas_call x2, Pallas kernels: 88.3 us -> 79.7 us  [block(): pl.pallas_call(functools.partial(block_kernel, last), out_shape=out_shape...]
    pad x5 -> x0, local copies, waits for them, and re-layouts: 3.7 us -> none  [the longest x1 1.09 us: per_device(): wp = jnp.pad(w_project, ((0, HP - HID), (0, 0)))]
    unnamed x11 -> x6, local copies, waits for them, and re-layouts: 6.57 us -> 5.74 us
  transfers between devices with their start and end apart: 1 -> 1, of which waited for: 0 -> 0; matrix products, arithmetic and copies ran while one was open for 3% -> 0% of each run, Pallas kernels for 32% -> 32%
where the time goes in v4:
time: 183 us
  Pallas kernels  167 us (91%)
  starting transfers between devices  9.44 us (5%)
  local copies, waits for them, and re-layouts  5.74 us (3%)
    pallas_call x2, Pallas kernels, block(): pl.pallas_call(functools.partial(block_kernel, last), out_shape=out_shape...  79.7 us
    pallas_call x1, Pallas kernels, fetch(): pl.pallas_call(fetch_kernel, out_shape=(jax.ShapeDtypeStruct((PEERS, SLOT...  44.2 us
    pallas_call x1, Pallas kernels, all_reduce(): pl.pallas_call(reduce_kernel, out_shape=(jax.ShapeDtypeStruct((CIN, HID),...  43.4 us
    all_to_all x1, starting transfers between devices, per_device(): lax.all_to_all(later.reshape(PEERS, 2, SLOT, 128), 'dp', split_axis=0, co...  9.44 us
    unnamed x6, local copies, waits for them, and re-layouts  5.74 us
  transfers between devices with their start and end apart: 1, of which 0 were waited for; matrix products, arithmetic and copies ran while one was open for 0% of the time, Pallas kernels for 32%

profile of v4, /device:TPU:1, one launch (start us, length us, event | category | flops | bytes accessed | tf_op | source)
XLA Modules:
  0.0 183.2 jit_solution(6244867767575287000)
XLA Ops:
  0.6 44.2 %fetch_frames.1 = (bf16[32,176,128]{2,1,0:T(8,128)(2,1)}, bf16[64,176,128]{2,1,0:T(8,128)(2,1)}) custom-call(s32[1,36]{1,0:T(1,128)} %bitcast.14, s32[1,36]{1,0:T(1,128)} %bitcast.12, s32[1,36]{1,0:T(1,128)} %bitcast.13, bf16[8,81,24,232]{3,2,1,0:T(8,128)(2,1)} %bitcast.9, bf16[8,512]{1,0:T(8,128)(2,1)} %ins_ref.1), custom_call_target="tpu_custom_call" | custom-call | tf_op jit(solution)/shard_map/fetch_frames/pallas_call | solution.py:119
  44.9 9.4 %all-to-all-start = ((bf16[32,2,176,128]{3,2,1,0:T(8,128)(2,1)}), bf16[32,2,176,128]{3,2,1,0:T(8,128)(2,1)S(1)}, u32[]{:S(2)}, u32[]{:S(2)}) async-start(bf16[32,2,176,128]{3,2,1,0:T(8,128)(2,1)} %bitcast.11), calls=%async_computation | async-start | bytes 5767168 | tf_op jit(solution)/shard_map/all_to_all | solution.py:492
  54.3 58.9 %early_frames.1 = (bf16[256,1408]{1,0:T(8,128)(2,1)}, f32[11,72,128]{2,1,0:T(8,128)}, bf16[1408,384]{1,0:T(8,128)(2,1)}, bf16[384,1408]{1,0:T(8,128)(2,1)}, f32[...) custom-call(s32[36]{0:T(128)} %bitcast.15, ...), custom_call_target="tpu_custom_call" | custom-call | flops 20000000000 | bytes 200000000 | tf_op jit(solution)/shard_map/early_frames/pallas_call | solution.py:350
  113.2 0.0 all-to-all-done
  113.2 0.0 copy-start
  113.2 1.6 copy-done
  114.8 20.8 %late_frames.1 = (bf16[36,81,384]{2,1,0:T(8,128)(2,1)}, bf16[10240,128]{1,0:T(8,128)(2,1)}) custom-call(s32[36]{0:T(128)} %bitcast.16, bf16[32,176,128]{2,1,0:T(8,128)(2,1)} %get-tuple-element.23.refs_1_, bf16[36,81,384]{2,1,0:T(8,128)(2,1)} %bitcast.18, bf16[512,768]{1,0:T(8,128)(2,1)} %refs_3_.3, ...), custom_call_target="tpu_custom_call", output_to_operand_aliasing={{0}: (14, {})} | custom-call | flops 20000000000 | bytes 200000000 | tf_op jit(solution)/shard_map/late_frames/pallas_call | solution.py:350
  135.6 43.4 %grad_sum.1 = (f32[232,1392]{1,0:T(8,128)S(1)}, f32[9,1392]{1,0:T(8,128)S(1)}, f32[1392,384]{1,0:T(8,128)S(1)}, f32[512,768]{1,0:T(8,128)S(1)}) custom-call(bf16[10240,128]{1,0:T(8,128)(2,1)} %get-tuple-element.36.g_ref), custom_call_target="tpu_custom_call" | custom-call | tf_op jit(solution)/shard_map/grad_sum/pallas_call | solution.py:476
  179.0 1.1 copy.21
  180.1 0.6 copy.22
  180.7 1.3 copy.23
  182.1 1.1 copy.24
Async XLA Ops:
  44.9 68.3 %all-to-all-start = ((bf16[32,2,176,128]{3,2,1,0:T(8,128)(2,1)}), bf16[32,2,176,128]{3,2,1,0:T(8,128)(2,1)S(1)}, u32[]{:S(2)}, u32[]{:S(2)}) async-start(bf16[32,2,176,128]{3,2,1,0:T(8,128)(2,1)} %bitcast.11), calls=%async_computation | async-start | bytes 5767168 | tf_op jit(solution)/shard_map/all_to_all | solution.py:492
  113.2 1.6 copy-start

commit v5 on v4

--- a/solution.py
+++ b/solution.py
@@ -350,7 +350,7 @@
     return pl.pallas_call(
         functools.partial(block_kernel, last),
         out_shape=out_shape, in_specs=in_specs, out_specs=out_specs, scratch_shapes=scratch, input_output_aliases=aliases,
-        compiler_params=pltpu.CompilerParams(vmem_limit_bytes=61 * 2**20),
+        compiler_params=pltpu.CompilerParams(vmem_limit_bytes=63 * 2**20),
         cost_estimate=pl.CostEstimate(flops=2 * 10**10, bytes_accessed=2 * 10**8, transcendentals=8 * 10**6),
         name="late_frames" if last else "early_frames",
     )(owner, *arrays)
@@ -377,7 +377,7 @@
     return other
 
 
-def reduce_kernel(g_ref, ge_ref, gk_ref, gp_ref, gf_ref, total, part, r0, r1, r2, r3, send, recv):
+def reduce_kernel(g_ref, sum_ref, total, part, r0, r1, r2, r3, send, recv):
     at = place()
     barrier = pltpu.get_barrier_semaphore()
     peers = [shifted(at, "core", 1)] + [shifted(at, a, d) for a in "xyz" for d in (1, 2, 3)]
@@ -420,34 +420,33 @@
                 for d in (1, 2, 3):
                     mine = mine + prev[d - 1, pl.ds(pb, have)].astype(f32)
             part[stage - 1, pl.ds(base, have)] = mine.astype(bf16)
-            block = have // 4
             state[s] = []
             for d in (1, 2, 3):
                 peer = shifted(at, axis, d)
-                state[s].append(push(part.at[stage - 1, span(base, peer[axis], block)],
-                                     land[stage].at[d - 1, pl.ds(base // 4 ** stage, block)], stage, s, d - 1, peer))
+                if stage == 3:
+                    src, dst = part.at[2, pl.ds(base, have)], r3.at[d - 1, pl.ds(base // 16, have)]
+                else:
+                    block = have // 4
+                    src = part.at[stage - 1, span(base, peer[axis], block)]
+                    dst = land[stage].at[d - 1, pl.ds(base // 4 ** stage, block)]
+                state[s].append(push(src, dst, stage, s, d - 1, peer))
     where = []
     for s, r in enumerate(PIECES):
         for c in state[s]:
             c.wait_recv()
-        base = STARTS[s] // 2
-        mine = part[2, span(base, at[ORDERS[s][2]], r)].astype(f32)
-        for d in (1, 2, 3):
-            mine = mine + r3[d - 1, pl.ds(base // 64, r)].astype(f32)
+        base, have = STARTS[s] // 2, 4 * r
+        own = part[2, pl.ds(base, have)].astype(f32)
+        near, far, back = [r3[d, pl.ds(base // 16, have)].astype(f32) for d in range(3)]
         a1, a2, a3 = ORDERS[s]
-        index = ((at["core"] * 4 + at[a1]) * 4 + at[a2]) * 4 + at[a3]
-        where.append(index)
-        total[span(STARTS[s], index, r)] = mine.astype(bf16)
+        where.append((at["core"] * 4 + at[a1]) * 4 + at[a2])
+        total[span(STARTS[s], where[s], have)] = ((own + far) + (near + back)).astype(bf16)
         state[s] = []
-        for d in (1, 2, 3):
-            sl = span(STARTS[s], index, r)
-            state[s].append(push(total.at[sl], total.at[sl], 4, s, d - 1, shifted(at, a3, d)))
     for stage in (5, 6, 7):
         for s, r in enumerate(PIECES):
             for c in state[s]:
                 c.wait_recv()
             rows = r * 4 ** (stage - 4)
-            index = where[s] // 4 ** (stage - 4)
+            index = where[s] // 4 ** (stage - 5)
             sl = span(STARTS[s], index, rows)
             state[s] = []
             if stage == 7:
@@ -461,6 +460,10 @@
             c.wait_recv()
     for c in waits:
         c.wait_send()
+    sum_ref[...] = total[...]
+
+
+def spread_kernel(total, ge_ref, gk_ref, gp_ref, gf_ref):
     for lt in range(11):
         w = min(128, HID - lt * 128)
         ge_ref[:, lt * 128:lt * 128 + w] = total[GE + lt * 240:GE + lt * 240 + 240].astype(f32)[:CIN, :w]
@@ -473,17 +476,20 @@
 
 def all_reduce(g):
     V = pl.BlockSpec(memory_space=pltpu.VMEM)
+    total = pl.pallas_call(
+        reduce_kernel, out_shape=jax.ShapeDtypeStruct((GR, 128), bf16), in_specs=[V], out_specs=V,
+        scratch_shapes=[pltpu.VMEM((GR, 128), bf16), pltpu.VMEM((3, GR // 2, 128), bf16), pltpu.VMEM((GR // 2, 128), bf16),
+                        pltpu.VMEM((3, GR // 8, 128), bf16), pltpu.VMEM((3, GR // 32, 128), bf16), pltpu.VMEM((3, GR // 32, 128), bf16),
+                        pltpu.SemaphoreType.DMA((8, 3, 3)), pltpu.SemaphoreType.DMA((8, 3, 3))],
+        compiler_params=pltpu.CompilerParams(vmem_limit_bytes=32 * 2**20, collective_id=1, has_side_effects=True),
+        name="grad_sum",
+    )(g)
     return pl.pallas_call(
-        reduce_kernel,
+        spread_kernel,
         out_shape=(jax.ShapeDtypeStruct((CIN, HID), f32), jax.ShapeDtypeStruct((9, HID), f32),
                    jax.ShapeDtypeStruct((HID, COUT), f32), jax.ShapeDtypeStruct((EMB, 2 * COUT), f32)),
-        in_specs=[V], out_specs=(V,) * 4,
-        scratch_shapes=[pltpu.VMEM((GR, 128), bf16), pltpu.VMEM((3, GR // 2, 128), bf16), pltpu.VMEM((GR // 2, 128), bf16),
-                        pltpu.VMEM((3, GR // 8, 128), bf16), pltpu.VMEM((3, GR // 32, 128), bf16), pltpu.VMEM((3, GR // 128, 128), bf16),
-                        pltpu.SemaphoreType.DMA((8, 3, 3)), pltpu.SemaphoreType.DMA((8, 3, 3))],
-        compiler_params=pltpu.CompilerParams(vmem_limit_bytes=48 * 2**20, collective_id=1, has_side_effects=True),
-        name="grad_sum",
-    )(g)
+        in_specs=[V], out_specs=(V,) * 4, compiler_params=pltpu.CompilerParams(vmem_limit_bytes=32 * 2**20), name="grad_spread",
+    )(total)
 
 
 def per_device(replay, instructions, owners, episode_rows, frame_steps, w_expand, dw_kernel, w_project, film_weight, token_grad):

time: 183 us -> 178 us (0.973)
  local copies, waits for them, and re-layouts: 5.74 us -> 1.73 us
  Pallas kernels: 167 us -> 165 us
    unnamed x6 -> x2, local copies, waits for them, and re-layouts: 5.74 us -> 1.73 us
    pallas_call x1 -> x2, Pallas kernels: 43.4 us -> 41.3 us  [the longest x1 38.9 us: all_reduce(): pl.pallas_call(reduce_kernel, out_shape=jax.ShapeDtypeStruct((GR, 128), b...]
  transfers between devices with their start and end apart: 1 -> 1, of which waited for: 0 -> 0; matrix products, arithmetic and copies ran while one was open for 0% -> 0% of each run, Pallas kernels for 32% -> 33%
where the time goes in v5:
time: 178 us; the launch traced here: 177 us
  Pallas kernels  165 us (93%)
  starting transfers between devices  9.49 us (5%)
    pallas_call x2, Pallas kernels, block(): pl.pallas_call(functools.partial(block_kernel, last), out_shape=out_shape...  79.7 us
    pallas_call x1, Pallas kernels, fetch(): pl.pallas_call(fetch_kernel, out_shape=(jax.ShapeDtypeStruct((PEERS, SLOT...  44.4 us
    pallas_call x1, Pallas kernels, all_reduce(): pl.pallas_call(reduce_kernel, out_shape=jax.ShapeDtypeStruct((GR, 128), b...  38.9 us
    all_to_all x1, starting transfers between devices, per_device(): lax.all_to_all(later.reshape(PEERS, 2, SLOT, 128), 'dp', split_axis=0, co...  9.49 us
  transfers between devices with their start and end apart: 1, of which 0 were waited for; matrix products, arithmetic and copies ran while one was open for 0% of the time, Pallas kernels for 33%

profile of v5, /device:TPU:1, one launch (start us, length us, event | category | flops | bytes accessed | tf_op | source)
XLA Modules:
  0.0 177.3 jit_solution(3672599787307614249)
XLA Ops:
  0.6 44.4 %fetch_frames.1 = (bf16[32,176,128]{2,1,0:T(8,128)(2,1)}, bf16[64,176,128]{2,1,0:T(8,128)(2,1)}) custom-call(s32[1,36]{1,0:T(1,128)} %bitcast.13, s32[1,36]{1,0:T(1,128)} %bitcast.11, s32[1,36]{1,0:T(1,128)} %bitcast.12, bf16[8,81,24,232]{3,2,1,0:T(8,128)(2,1)} %bitcast.9, bf16[8,512]{1,0:T(8,128)(2,1)} %ins_ref.1), custom_call_target="tpu_custom_call" | custom-call | tf_op jit(solution)/shard_map/fetch_frames/pallas_call | solution.py:119
  45.1 9.5 %all-to-all-start = ((bf16[32,2,176,128]{3,2,1,0:T(8,128)(2,1)}), bf16[32,2,176,128]{3,2,1,0:T(8,128)(2,1)}, u32[]{:S(2)}, u32[]{:S(2)}) async-start(bf16[32,2,176,128]{3,2,1,0:T(8,128)(2,1)} %bitcast.10), calls=%async_computation | async-start | bytes 5767168 | tf_op jit(solution)/shard_map/all_to_all | solution.py:498
  54.6 58.9 %early_frames.1 = (bf16[256,1408]{1,0:T(8,128)(2,1)}, f32[11,72,128]{2,1,0:T(8,128)}, bf16[1408,384]{1,0:T(8,128)(2,1)}, bf16[384,1408]{1,0:T(8,128)(2,1)}, f32[...) custom-call(s32[36]{0:T(128)} %bitcast.14, ...), custom_call_target="tpu_custom_call" | custom-call | flops 20000000000 | bytes 200000000 | tf_op jit(solution)/shard_map/early_frames/pallas_call | solution.py:350
  113.5 0.0 all-to-all-done
  113.5 20.8 %late_frames.1 = (bf16[36,81,384]{2,1,0:T(8,128)(2,1)}, bf16[10240,128]{1,0:T(8,128)(2,1)}) custom-call(s32[36]{0:T(128)} %bitcast.15, bf16[32,176,128]{2,1,0:T(8,128)(2,1)} %get-tuple-element.23.refs_1_, bf16[36,81,384]{2,1,0:T(8,128)(2,1)} %bitcast.17, bf16[512,768]{1,0:T(8,128)(2,1)} %refs_3_.3, ...), custom_call_target="tpu_custom_call", output_to_operand_aliasing={{0}: (14, {})} | custom-call | flops 20000000000 | bytes 200000000 | tf_op jit(solution)/shard_map/late_frames/pallas_call | solution.py:350
  134.3 0.0 copy-start
  134.3 1.7 copy-done
  136.1 38.9 %grad_sum.1.total = bf16[10240,128]{1,0:T(8,128)(2,1)S(1)} custom-call(bf16[10240,128]{1,0:T(8,128)(2,1)S(1)} %copy-done), custom_call_target="tpu_custom_call" | custom-call | tf_op jit(solution)/shard_map/grad_sum/pallas_call | solution.py:479
  175.0 2.4 %grad_spread.1 = (f32[232,1392]{1,0:T(8,128)}, f32[9,1392]{1,0:T(8,128)}, f32[1392,384]{1,0:T(8,128)}, f32[512,768]{1,0:T(8,128)}) custom-call(bf16[10240,128]{1,0:T(8,128)(2,1)S(1)} %grad_sum.1.total), custom_call_target="tpu_custom_call" | custom-call | tf_op jit(solution)/shard_map/grad_spread/pallas_call | solution.py:487
Async XLA Ops:
  45.1 68.4 %all-to-all-start = ((bf16[32,2,176,128]{3,2,1,0:T(8,128)(2,1)}), bf16[32,2,176,128]{3,2,1,0:T(8,128)(2,1)}, u32[]{:S(2)}, u32[]{:S(2)}) async-start(bf16[32,2,176,128]{3,2,1,0:T(8,128)(2,1)} %bitcast.10), calls=%async_computation | async-start | bytes 5767168 | tf_op jit(solution)/shard_map/all_to_all | solution.py:498
  134.3 1.7 copy-start

commit v6 on v5

--- a/solution.py
+++ b/solution.py
@@ -350,7 +350,7 @@
     return pl.pallas_call(
         functools.partial(block_kernel, last),
         out_shape=out_shape, in_specs=in_specs, out_specs=out_specs, scratch_shapes=scratch, input_output_aliases=aliases,
-        compiler_params=pltpu.CompilerParams(vmem_limit_bytes=63 * 2**20),
+        compiler_params=pltpu.CompilerParams(vmem_limit_bytes=46 * 2**20),
         cost_estimate=pl.CostEstimate(flops=2 * 10**10, bytes_accessed=2 * 10**8, transcendentals=8 * 10**6),
         name="late_frames" if last else "early_frames",
     )(owner, *arrays)

time: 178 us -> 189 us (1.062)
  local copies, waits for them, and re-layouts: 1.73 us -> 15.2 us
  Pallas kernels: 165 us -> 163 us
    unnamed x2 -> x38, local copies, waits for them, and re-layouts: 1.73 us -> 15.2 us
    pallas_call x2, Pallas kernels: 79.7 us -> 76.8 us  [block(): pl.pallas_call(functools.partial(block_kernel, last), out_shape=out_shape...]
  transfers between devices with their start and end apart: 1 -> 1, of which waited for: 0 -> 0; matrix products, arithmetic and copies ran while one was open for 0% -> 0% of each run, Pallas kernels for 33% -> 30%
where the time goes in v6:
time: 189 us; the launch traced here: 188 us
  Pallas kernels  163 us (86%)
  local copies, waits for them, and re-layouts  15.2 us (8%)
  starting transfers between devices  9.6 us (5%)
    pallas_call x2, Pallas kernels, block(): pl.pallas_call(functools.partial(block_kernel, last), out_shape=out_shape...  76.8 us
    pallas_call x1, Pallas kernels, fetch(): pl.pallas_call(fetch_kernel, out_shape=(jax.ShapeDtypeStruct((PEERS, SLOT...  44.4 us
    pallas_call x1, Pallas kernels, all_reduce(): pl.pallas_call(reduce_kernel, out_shape=jax.ShapeDtypeStruct((GR, 128), b...  39 us
    unnamed x38, local copies, waits for them, and re-layouts  15.2 us
    all_to_all x1, starting transfers between devices, per_device(): lax.all_to_all(later.reshape(PEERS, 2, SLOT, 128), 'dp', split_axis=0, co...  9.6 us
  transfers between devices with their start and end apart: 1, of which 0 were waited for; matrix products, arithmetic and copies ran while one was open for 0% of the time, Pallas kernels for 30%

profile of v6, /device:TPU:1, one launch (start us, length us, event | category | flops | bytes accessed | tf_op | source)
XLA Modules:
  0.0 188.1 jit_solution(12943614782917786287)
XLA Ops:
  0.6 44.4 %fetch_frames.1 = (bf16[32,176,128]{2,1,0:T(8,128)(2,1)}, bf16[64,176,128]{2,1,0:T(8,128)(2,1)}) custom-call(s32[1,36]{1,0:T(1,128)} %bitcast.9, s32[1,36]{1,0:T(1,128)} %bitcast.14, s32[1,36]{1,0:T(1,128)} %bitcast.15, bf16[8,81,24,232]{3,2,1,0:T(8,128)(2,1)} %bitcast.12, bf16[8,512]{1,0:T(8,128)(2,1)} %ins_ref.1), custom_call_target="tpu_custom_call" | custom-call | tf_op jit(solution)/shard_map/fetch_frames/pallas_call | solution.py:119
  45.1 0.0 copy-start.1
  45.1 0.0 copy-start.3
  45.1 0.0 copy-start.4
  45.1 0.0 copy-start.6
  45.1 9.6 %all-to-all-start = ((bf16[32,2,176,128]{3,2,1,0:T(8,128)(2,1)}), bf16[32,2,176,128]{3,2,1,0:T(8,128)(2,1)}, u32[]{:S(2)}, u32[]{:S(2)}) async-start(bf16[32,2,176,128]{3,2,1,0:T(8,128)(2,1)} %bitcast.13), calls=%async_computation | async-start | bytes 5767168 | tf_op jit(solution)/shard_map/all_to_all | solution.py:498
  54.7 0.0 copy-done.1
  54.7 0.0 copy-done.3
  54.7 0.0 copy-done.4
  54.8 0.0 copy-done.6
  54.8 0.0 copy-start.5
  54.8 1.1 copy-done.5
  55.9 56.9 %early_frames.1 = (bf16[256,1408]{1,0:T(8,128)(2,1)S(1)}, f32[11,72,128]{2,1,0:T(8,128)S(1)}, bf16[1408,384]{1,0:T(8,128)(2,1)S(1)}, bf16[384,1408]{1,0:T(8,128)...) custom-call(s32[36]{0:T(128)S(1)} %bitcast.10, ...), custom_call_target="tpu_custom_call" | custom-call | flops 20000000000 | bytes 200000000 | tf_op jit(solution)/shard_map/early_frames/pallas_call | solution.py:350
  112.8 0.0 copy-start.7
  112.8 1.1 copy-done.7
  113.9 1.0 copy-done.9
  114.9 1.0 copy-done.11
  115.9 0.9 copy-done.13
  116.7 0.8 copy-done.15
  117.5 0.8 copy-done.17
  118.3 0.0 all-to-all-done
  118.3 0.0 copy-done.2
  118.3 1.4 copy-done.8
  119.6 1.2 copy-done.10
  120.9 1.2 copy-done.12
  122.1 1.1 copy-done.14
  123.2 1.0 copy-done.16
  124.2 1.0 copy-done.18
  125.2 19.8 %late_frames.1 = (bf16[36,81,384]{2,1,0:T(8,128)(2,1)}, bf16[10240,128]{1,0:T(8,128)(2,1)}) custom-call(s32[36]{0:T(128)S(1)} %bitcast.11, bf16[32,176,128]{2,1,0:T(8,128)(2,1)S(1)} %copy-done.2, bf16[36,81,384]{2,1,0:T(8,128)(2,1)} %bitcast.17, bf16[512,768]{1,0:T(8,128)(2,1)S(1)} %copy-done.4, ...), custom_call_target="tpu_custom_call", output_to_operand_aliasing={{0}: (14, {})} | custom-call | flops 20000000000 | bytes 200000000 | tf_op jit(solution)/shard_map/late_frames/pallas_call | solution.py:350
  145.0 1.7 copy-done
  146.8 39.0 %grad_sum.1.total = bf16[10240,128]{1,0:T(8,128)(2,1)S(1)} custom-call(bf16[10240,128]{1,0:T(8,128)(2,1)S(1)} %copy-done), custom_call_target="tpu_custom_call" | custom-call | tf_op jit(solution)/shard_map/grad_sum/pallas_call | solution.py:479
  185.8 2.4 %grad_spread.1 = (f32[232,1392]{1,0:T(8,128)}, f32[9,1392]{1,0:T(8,128)}, f32[1392,384]{1,0:T(8,128)}, f32[512,768]{1,0:T(8,128)}) custom-call(bf16[10240,128]{1,0:T(8,128)(2,1)S(1)} %grad_sum.1.total), custom_call_target="tpu_custom_call" | custom-call | tf_op jit(solution)/shard_map/grad_spread/pallas_call | solution.py:487
  (13 shorter events, 0.0 us)
Async XLA Ops:
  45.1 9.7 %copy-start.1 = (s32[36,1]{0,1:T(1,128)S(1)}, s32[36,1]{0,1:T(1,128)}, u32[]{:S(2)}) copy-start(s32[36,1]{0,1:T(1,128)} %param.12) | copy-start | bytes 436
  45.1 9.7 %copy-start.3 = (bf16[1392,384]{1,0:T(8,128)(2,1)S(1)}, bf16[1392,384]{1,0:T(8,128)(2,1)}, u32[]{:S(2)}) copy-start(bf16[1392,384]{1,0:T(8,128)(2,1)} %refs_6_.1) | copy-start | bytes 3207172
  45.1 9.7 %copy-start.4 = (bf16[512,768]{1,0:T(8,128)(2,1)S(1)}, bf16[512,768]{1,0:T(8,128)(2,1)}, u32[]{:S(2)}) copy-start(bf16[512,768]{1,0:T(8,128)(2,1)} %refs_3_.3) | copy-start | bytes 2359300
  45.1 9.7 %copy-start.6 = (f32[9,1392]{1,0:T(8,128)S(1)}, f32[9,1392]{1,0:T(8,128)}, u32[]{:S(2)}) copy-start(f32[9,1392]{1,0:T(8,128)} %refs_5_.1) | copy-start | bytes 150340
  45.1 73.2 %all-to-all-start = ((bf16[32,2,176,128]{3,2,1,0:T(8,128)(2,1)}), bf16[32,2,176,128]{3,2,1,0:T(8,128)(2,1)}, u32[]{:S(2)}, u32[]{:S(2)}) async-start(bf16[32,2,176,128]{3,2,1,0:T(8,128)(2,1)} %bitcast.13), calls=%async_computation | async-start | bytes 5767168 | tf_op jit(solution)/shard_map/all_to_all | solution.py:498
  54.8 1.1 copy-start.5
  55.9 62.4 %copy-start.2 = (bf16[32,176,128]{2,1,0:T(8,128)(2,1)S(1)}, bf16[32,176,128]{2,1,0:T(8,128)(2,1)}, u32[]{:S(2)}) copy-start(bf16[32,176,128]{2,1,0:T(8,128)(2,1)} %get-tuple-element.23.refs_1_) | copy-start | bytes 4325380
  112.8 1.1 copy-start.7
  113.9 1.0 copy-start.9
  114.9 1.0 copy-start.11
  115.9 0.9 copy-start.13
  116.7 0.8 copy-start.15
  117.5 0.8 copy-start.17
  118.3 1.4 copy-start.8
  119.6 1.2 copy-start.10
  120.9 1.2 copy-start.12
  122.1 1.1 copy-start.14
  123.2 1.0 copy-start.16
  124.2 1.0 copy-start.18
  145.0 1.7 copy-start
